TPU v7x, 512 devices: a whole 4x4x16 slice. The times are simulated.
512 devices in a mesh: city: 16 (over x, y), tile: 32 (over z, core).
Axes of the slice: x: 4, y: 4, z: 16, core: 2. Of those that a mesh axis runs over, the one named last changes fastest.
Arguments:
- right_side: float32 [2, 1048576], P(None, ('city', 'tile')), may hold values from -25 to 25
- noise_var: float32 [1048576], P(('city', 'tile')), may hold values from 0.1 to 1
- coords: float32 [2, 1048576], P(None, 'city'), may hold values from 0 to 641
- counts: int32 [512], P(('city', 'tile')), may hold values from 1024 to 2048
- pair_list: int32 [512, 5, 3], P(('city', 'tile')), may hold values from 0 to 31, as said below
Outputs:
- solution_field: float32 [2, 1048576], P(None, ('city', 'tile'))
- residual: float32 [2, 1048576], P(None, ('city', 'tile'))
Inputs may be any that keep to these rules, and one draw needn't show every extreme that they name: `pair_list`: columns are first tile, second tile (both indices within a city) and kind: 0 an empty slot (tiles 0), 1 both tiles in the owner's city, 2 the second tile in the next city, 3 the second tile in the previous city. Every unordered pair of tiles of a city that is listed appears once in that city (a tile with itself too); a pair (a, b) of kind 2 in city c appears as (b, a) of kind 3 in city c + 1. A city lists at most 65 live pairs, at most one of kind 2 and one of kind 3. A device holds at most 5 live pairs, and some device holds that many. A tile is the first tile of, or the second tile of a kind 1 pair with a != b, in at most 3 live pairs of its city, and some tile of every city in exactly 3.
All inputs are finite; a program needn't handle non-finite values.
Results may differ from a plain program's by a relative error of at most 0.025.
Values may be sent and summed in bfloat16 or wider, within the bound.
No kernel may reach another device: no remote copies, remote signals or barrier semaphores. Data moves between devices by JAX's collectives and lax.ppermute only.
A program may use at most 64 MiB of HBM per device.

v0:
```python
import jax
import jax.numpy as jnp
from jax import lax
from jax.sharding import PartitionSpec as P

ITERS = 3


def padded(array, sides, width):
    for axis, dim in sides:
        size, length = (lax.axis_size(axis), array.shape[dim])
        up = [(i, (i + 1) % size) for i in range(size - 1)]
        down = [(j, i) for i, j in up]
        last = lax.slice_in_dim(array, length - width, length, axis=dim)
        leading = lax.slice_in_dim(array, 0, width, axis=dim)
        before = lax.ppermute(last, axis, up)
        after = lax.ppermute(leading, axis, down)
        array = jnp.concatenate([before, array, after], axis=dim)
    return array


def wendland(near_pts, far_pts):
    across = near_pts[0][:, None] - far_pts[0][None, :]
    along_y = near_pts[1][:, None] - far_pts[1][None, :]
    reach = jnp.sqrt(across * across + along_y * along_y)
    inside = jnp.maximum(1.0 - reach, 0.0)
    square = inside * inside
    return square * square * (4.0 * reach + 1.0)


def to_bfloat(values):
    return lax.optimization_barrier(values.astype(jnp.bfloat16)).astype(jnp.float32)


def body(right_side, noise_var, coords, counts, pair_list):
    tile_count = lax.axis_size("tile")
    tile_len = right_side.shape[1]
    columns = right_side.shape[0]
    row_block = min(512, tile_len)
    valid_mask = (jnp.arange(tile_len) < counts[0]).astype(jnp.float32)
    noise_eff = jnp.where(valid_mask > 0, noise_var, 1.0)
    wide_coords = padded(coords, (("city", 1),), tile_count * tile_len)
    my_pairs = pair_list[0]
    slot_count = my_pairs.shape[0]

    def far_place(second_tile, pair_kind):
        city_shift = (pair_kind == 2).astype(jnp.int32) - (pair_kind == 3).astype(jnp.int32)
        return second_tile + tile_count * (1 + city_shift)

    residual = right_side * valid_mask[None, :]
    direction = residual
    solution_field = jnp.zeros_like(residual)
    norm_now = lax.psum(jnp.sum(residual * residual, axis=1), ("city", "tile"))
    for iteration in range(ITERS):
        own_dirs = direction.astype(jnp.bfloat16)
        city_dirs = lax.all_gather(own_dirs[None], "tile", axis=0, tiled=True)
        wide_dirs = padded(city_dirs, (("city", 0),), tile_count)

        def add_pair(slot_id, buffer):
            pair_row = lax.dynamic_index_in_dim(my_pairs, slot_id, 0, False)
            first_tile = pair_row[0]
            second_tile = pair_row[1]
            pair_kind = pair_row[2]
            far_tile = far_place(second_tile, pair_kind)

            def compute(current):
                near_pts = lax.dynamic_slice_in_dim(
                    wide_coords, (tile_count + first_tile) * tile_len, tile_len, 1
                )
                far_pts = lax.dynamic_slice_in_dim(wide_coords, far_tile * tile_len, tile_len, 1)
                near_vec = lax.dynamic_index_in_dim(city_dirs, first_tile, 0, False)
                far_vec = lax.dynamic_index_in_dim(wide_dirs, far_tile, 0, False)
                pieces = []
                back_sum = jnp.zeros((columns, tile_len), jnp.float32)
                for offset in range(0, tile_len, row_block):
                    kernel = wendland(near_pts[:, offset : offset + row_block], far_pts).astype(
                        jnp.bfloat16
                    )
                    pieces.append(
                        lax.dot_general(
                            far_vec,
                            kernel,
                            (((1,), (1,)), ((), ())),
                            preferred_element_type=jnp.float32,
                        )
                    )
                    back_sum = back_sum + jnp.dot(
                        near_vec[:, offset : offset + row_block],
                        kernel,
                        preferred_element_type=jnp.float32,
                    )
                to_near = to_bfloat(jnp.concatenate(pieces, axis=1))
                both_ways = ((pair_kind == 1) & (first_tile != second_tile)).astype(jnp.float32)
                to_far = to_bfloat(back_sum) * both_ways
                old_near = lax.dynamic_index_in_dim(current, first_tile, 0, False)
                current = lax.dynamic_update_index_in_dim(
                    current, old_near + to_near, first_tile, 0
                )
                old_far = lax.dynamic_index_in_dim(current, second_tile, 0, False)
                return lax.dynamic_update_index_in_dim(current, old_far + to_far, second_tile, 0)

            return lax.cond(pair_kind > 0, compute, lambda unchanged: unchanged, buffer)

        buffer = lax.fori_loop(
            0, slot_count, add_pair, jnp.zeros((tile_count, columns, tile_len), jnp.float32)
        )
        arrived = lax.all_to_all(
            buffer.astype(jnp.bfloat16), "tile", split_axis=0, concat_axis=0, tiled=True
        ).astype(buffer.dtype)
        summed = jnp.sum(arrived, axis=0)
        applied = valid_mask[None, :] * summed + noise_eff[None, :] * direction
        curvature = lax.psum(jnp.sum(direction * applied, axis=1), ("city", "tile"))
        step_size = norm_now / curvature
        solution_field = solution_field + step_size[:, None] * direction
        residual = residual - step_size[:, None] * applied
        if iteration + 1 < ITERS:
            norm_next = lax.psum(jnp.sum(residual * residual, axis=1), ("city", "tile"))
        if iteration + 1 < ITERS:
            direction = residual + (norm_next / norm_now)[:, None] * direction
            norm_now = norm_next
    return (solution_field, residual)


def solution(mesh):
    placed = (
        P(None, ("city", "tile")),
        P(("city", "tile")),
        P(None, "city"),
        P(("city", "tile")),
        P(("city", "tile"), None, None),
    )
    return jax.shard_map(
        body,
        mesh=mesh,
        in_specs=placed,
        out_specs=(P(None, ("city", "tile")), P(None, ("city", "tile"))),
        check_vma=False,
    )
```

profile of v0, /device:TPU:1, one launch (start us, length us, event | category | flops | bytes accessed | tf_op | source)
XLA Modules:
  0.0 1235.6 jit_solution(6183938489834004527)
XLA Ops:
  0.6 5.0 collective-permute-start.2
  7.0 37.7 %all-gather.3 = bf16[32,2,2048]{2,1,0:T(2,128)(2,1)S(1)} all-gather(bf16[1,2,2048]{2,1,0:T(2,128)(2,1)S(1)} %convert_bitcast_fusion.2), channel_id=2, replica_groups=mesh['city'=16,'tile'=32] {'tile'}, dimensions={0}, use_global_device_ids=true | all-gather | bytes 270336 | tf_op jit(solution)/shard_map/all_gather | solution.py:56
  52.7 3.8 collective-permute-done.1
  58.8 9.0 collective-permute-done.3
  69.2 73.9 %while.48 = (s32[]{:T(128)}, f32[32,2,2048]{2,1,0:T(2,128)S(1)}, s32[5,3]{1,0:T(8,128)S(1)}, bf16[96,2,2048]{2,1,0:T(2,128)(2,1)S(1)}, f32[2,196608]{1,0:T(2,128...) while((s32[]{:T(128)}, f32[32,2,2048]{2,1,0:T(2,128)S(1)}, ...), condition=%wide.region_5.6_spmd, body=%wide.region_2.5_spmd.sunk | while | flops 142680096 | bytes 565899 | solution.py:104
  72.0 29.8 %conditional.6 = (f32[32,2,2048]{2,1,0:T(2,128)S(1)}) conditional(s32[]{:T(128)} %convert_element_type.323, f32[32,2,2048]{2,1,0:T(2,128)S(1)} %get-tuple-element.834, (s32[1,3]{1,0:T(1,128)S(1)}, f32[32,2,2048]{2,1,0:T(2,128)S(1)}, s32[]{:T(128)}, s32[]{:T(128)}, bf16[96,2,2048]{2,1,0:T(2,128)(2,1)S(1)}, /*index=5*/f32[2,196608]{1,0:T(2,128)S(1)}, ...), branch_computations={%region_3.3_spmd, %region_4.4_spmd} | conditional | flops 142680096 | bytes 565656 | solution.py:102
  104.5 29.8 %conditional.6 = (f32[32,2,2048]{2,1,0:T(2,128)S(1)}) conditional(s32[]{:T(128)} %convert_element_type.323, f32[32,2,2048]{2,1,0:T(2,128)S(1)} %get-tuple-element.834, (s32[1,3]{1,0:T(1,128)S(1)}, f32[32,2,2048]{2,1,0:T(2,128)S(1)}, s32[]{:T(128)}, s32[]{:T(128)}, bf16[96,2,2048]{2,1,0:T(2,128)(2,1)S(1)}, /*index=5*/f32[2,196608]{1,0:T(2,128)S(1)}, ...), branch_computations={%region_3.3_spmd, %region_4.4_spmd} | conditional | flops 142680096 | bytes 565656 | solution.py:102
  144.0 92.8 %all-to-all-start = ((bf16[32,2,2048]{2,1,0:T(2,128)(2,1)}), bf16[32,2,2048]{2,1,0:T(2,128)(2,1)S(1)}, u32[]{:S(2)}, u32[]{:S(2)}) async-start(bf16[32,2,2048]{2,1,0:T(2,128)(2,1)} %convert_element_type.228), calls=%async_computation | async-start | bytes 524288 | tf_op jit(solution)/shard_map/all_to_all | solution.py:107
  236.8 22.0 %all-to-all-done = bf16[32,2,2048]{2,1,0:T(2,128)(2,1)S(1)} async-done(((bf16[32,2,2048]{2,1,0:T(2,128)(2,1)}), bf16[32,2,2048]{2,1,0:T(2,128)(2,1)S(1)}, u32[]{:S(2)}, u32[]{:S(2)}) %all-to-all-start) | async-done | bytes 262176 | tf_op jit(solution)/shard_map/all_to_all | solution.py:107
  259.2 104.5 %all-reduce = (f32[2]{0:T(128)S(1)}, f32[2]{0:T(128)S(1)}) all-reduce(f32[2]{0:T(128)S(1)} %get-tuple-element.627, f32[2]{0:T(128)S(1)} %get-tuple-element.626), channel_id=1, replica_groups=mesh['city'=16,'tile'=32] {'city','tile'}, use_global_device_ids=true, to_apply=%region_1.2 | all-reduce | flops 4 | bytes 32 | tf_op jit(solution)/shard_map/psum | solution.py:53
  363.9 100.3 %psum.44 = f32[2]{0:T(128)S(1)} all-reduce(f32[2]{0:T(128)S(1)} %get-tuple-element.672), channel_id=1, replica_groups=mesh['city'=16,'tile'=32] {'city','tile'}, use_global_device_ids=true, to_apply=%region_10.11 | all-reduce | flops 2 | bytes 16 | tf_op jit(solution)/shard_map/psum | solution.py:117
  464.3 29.1 %all-gather.4 = bf16[32,2,2048]{2,1,0:T(2,128)(2,1)S(1)} all-gather(bf16[1,2,2048]{2,1,0:T(2,128)(2,1)S(1)} %get-tuple-element.670), channel_id=3, replica_groups=mesh['city'=16,'tile'=32] {'tile'}, dimensions={0}, use_global_device_ids=true | all-gather | bytes 270336 | tf_op jit(solution)/shard_map/all_gather | solution.py:56
  497.5 4.2 collective-permute-done.4
  501.7 3.8 collective-permute-done.5
  506.8 74.1 %while.49 = (s32[]{:T(128)}, f32[32,2,2048]{2,1,0:T(2,128)S(1)}, s32[5,3]{1,0:T(8,128)S(1)}, bf16[96,2,2048]{2,1,0:T(2,128)(2,1)S(1)}, f32[2,196608]{1,0:T(2,128...) while((s32[]{:T(128)}, f32[32,2,2048]{2,1,0:T(2,128)S(1)}, ...), condition=%wide.region_14.15_spmd, body=%wide.region_11.14_spmd.sunk | while | flops 142680096 | bytes 565899 | solution.py:104
  509.8 29.8 %conditional.7 = (f32[32,2,2048]{2,1,0:T(2,128)S(1)}) conditional(s32[]{:T(128)} %convert_element_type.326, f32[32,2,2048]{2,1,0:T(2,128)S(1)} %get-tuple-element.864, (s32[1,3]{1,0:T(1,128)S(1)}, f32[32,2,2048]{2,1,0:T(2,128)S(1)}, s32[]{:T(128)}, s32[]{:T(128)}, bf16[96,2,2048]{2,1,0:T(2,128)(2,1)S(1)}, /*index=5*/f32[2,196608]{1,0:T(2,128)S(1)}, ...), branch_computations={%region_12.12_spmd, %region_13.13_spmd} | conditional | flops 142680096 | bytes 565656 | solution.py:102
  527.3 2.8 fusion.51
  530.1 2.8 fusion.50
  532.9 2.8 fusion.49
  542.4 29.8 %conditional.7 = (f32[32,2,2048]{2,1,0:T(2,128)S(1)}) conditional(s32[]{:T(128)} %convert_element_type.326, f32[32,2,2048]{2,1,0:T(2,128)S(1)} %get-tuple-element.864, (s32[1,3]{1,0:T(1,128)S(1)}, f32[32,2,2048]{2,1,0:T(2,128)S(1)}, s32[]{:T(128)}, s32[]{:T(128)}, bf16[96,2,2048]{2,1,0:T(2,128)(2,1)S(1)}, /*index=5*/f32[2,196608]{1,0:T(2,128)S(1)}, ...), branch_computations={%region_12.12_spmd, %region_13.13_spmd} | conditional | flops 142680096 | bytes 565656 | solution.py:102
  559.9 2.8 fusion.51
  581.2 113.3 %all_to_all.15 = bf16[32,2,2048]{2,1,0:T(2,128)(2,1)S(1)} all-to-all(bf16[32,2,2048]{2,1,0:T(2,128)(2,1)S(1)} %convert_element_type.231), channel_id=1, replica_groups=mesh['city'=16,'tile'=32] {'tile'}, dimensions={0} | all-to-all | bytes 524288 | tf_op jit(solution)/shard_map/all_to_all | solution.py:107
  694.9 104.4 %psum.45 = f32[2]{0:T(128)S(1)} all-reduce(f32[2]{0:T(128)S(1)} %multiply_reduce_fusion.2), channel_id=1, replica_groups=mesh['city'=16,'tile'=32] {'city','tile'}, use_global_device_ids=true, to_apply=%region_17.18 | all-reduce | flops 2 | bytes 16 | tf_op jit(solution)/shard_map/psum | solution.py:112
  799.5 100.3 %psum.46 = f32[2]{0:T(128)S(1)} all-reduce(f32[2]{0:T(128)S(1)} %get-tuple-element.668), channel_id=1, replica_groups=mesh['city'=16,'tile'=32] {'city','tile'}, use_global_device_ids=true, to_apply=%region_19.20 | all-reduce | flops 2 | bytes 16 | tf_op jit(solution)/shard_map/psum | solution.py:117
  899.9 29.1 %all-gather.5 = bf16[32,2,2048]{2,1,0:T(2,128)(2,1)S(1)} all-gather(bf16[1,2,2048]{2,1,0:T(2,128)(2,1)S(1)} %get-tuple-element.666), channel_id=4, replica_groups=mesh['city'=16,'tile'=32] {'tile'}, dimensions={0}, use_global_device_ids=true | all-gather | bytes 270336 | tf_op jit(solution)/shard_map/all_gather | solution.py:56
  933.0 4.2 collective-permute-done.6
  937.3 3.8 collective-permute-done.7
  942.4 73.7 %while.50 = (s32[]{:T(128)}, f32[32,2,2048]{2,1,0:T(2,128)S(1)}, s32[5,3]{1,0:T(8,128)S(1)}, bf16[96,2,2048]{2,1,0:T(2,128)(2,1)S(1)}, f32[2,196608]{1,0:T(2,128...) while((s32[]{:T(128)}, f32[32,2,2048]{2,1,0:T(2,128)S(1)}, ...), condition=%wide.region_23.24_spmd, body=%wide.region_20.23_spmd.sunk | while | flops 142680096 | bytes 565899 | solution.py:104
  945.4 29.8 %conditional.8 = (f32[32,2,2048]{2,1,0:T(2,128)S(1)}) conditional(s32[]{:T(128)} %convert_element_type.329, f32[32,2,2048]{2,1,0:T(2,128)S(1)} %get-tuple-element.894, (s32[1,3]{1,0:T(1,128)S(1)}, f32[32,2,2048]{2,1,0:T(2,128)S(1)}, s32[]{:T(128)}, s32[]{:T(128)}, bf16[96,2,2048]{2,1,0:T(2,128)(2,1)S(1)}, /*index=5*/f32[2,196608]{1,0:T(2,128)S(1)}, ...), branch_computations={%region_21.21_spmd, %region_22.22_spmd} | conditional | flops 142680096 | bytes 565656 | solution.py:102
  978.0 29.8 %conditional.8 = (f32[32,2,2048]{2,1,0:T(2,128)S(1)}) conditional(s32[]{:T(128)} %convert_element_type.329, f32[32,2,2048]{2,1,0:T(2,128)S(1)} %get-tuple-element.894, (s32[1,3]{1,0:T(1,128)S(1)}, f32[32,2,2048]{2,1,0:T(2,128)S(1)}, s32[]{:T(128)}, s32[]{:T(128)}, bf16[96,2,2048]{2,1,0:T(2,128)(2,1)S(1)}, /*index=5*/f32[2,196608]{1,0:T(2,128)S(1)}, ...), branch_computations={%region_21.21_spmd, %region_22.22_spmd} | conditional | flops 142680096 | bytes 565656 | solution.py:102
  1016.4 113.3 %all_to_all.16 = bf16[32,2,2048]{2,1,0:T(2,128)(2,1)S(1)} all-to-all(bf16[32,2,2048]{2,1,0:T(2,128)(2,1)S(1)} %convert_element_type.234), channel_id=1, replica_groups=mesh['city'=16,'tile'=32] {'tile'}, dimensions={0} | all-to-all | bytes 524288 | tf_op jit(solution)/shard_map/all_to_all | solution.py:107
  1130.1 104.4 %psum.47 = f32[2]{0:T(128)S(1)} all-reduce(f32[2]{0:T(128)S(1)} %multiply_reduce_fusion), channel_id=1, replica_groups=mesh['city'=16,'tile'=32] {'city','tile'}, use_global_device_ids=true, to_apply=%region_26.27 | all-reduce | flops 2 | bytes 16 | tf_op jit(solution)/shard_map/psum | solution.py:112
  (190 shorter events, 166.5 us)
Async XLA Ops:
  0.6 58.1 %copy-start = (f32[2,65536]{1,0:T(2,128)S(1)}, f32[2,65536]{1,0:T(2,128)}, u32[]{:S(2)}) copy-start(f32[2,65536]{1,0:T(2,128)} %param.19) | copy-start | bytes 1572868
  0.6 57.0 %collective-permute-start.2 = (f32[2,65536]{1,0:T(2,128)}, f32[2,65536]{1,0:T(2,128)}, u32[]{:S(2)}, u32[]{:S(2)}) collective-permute-start(f32[2,65536]{1,0:T(2,128)} %param.19), channel_id=1, source_target_pairs={{0,32},{32,64},{64,96},{96,128},{128,160},{160,192},{192,224},{224... | collective-permute-start | bytes 1572872 | tf_op jit(solution)/shard_map/ppermute | solution.py:16
  44.7 7.9 collective-permute-start
  47.2 9.3 collective-permute-start.1
  48.5 19.4 %collective-permute-start.3 = (f32[2,65536]{1,0:T(2,128)}, f32[2,65536]{1,0:T(2,128)}, u32[]{:S(2)}, u32[]{:S(2)}) collective-permute-start(f32[2,65536]{1,0:T(2,128)} %param.19), channel_id=1, source_target_pairs={{32,0},{64,32},{96,64},{128,96},{160,128},{192,160},{224,192},{256... | collective-permute-start | bytes 1572872 | tf_op jit(solution)/shard_map/ppermute | solution.py:17
  69.2 167.6 %copy-start.3 = (f32[2048]{0:T(1024)S(1)}, f32[2048]{0:T(1024)}, u32[]{:S(2)}) copy-start(f32[2048]{0:T(1024)} %param.18) | copy-start | bytes 24580
  143.1 115.9 %copy-start.1 = (f32[2,2048]{1,0:T(2,128)S(1)}, f32[2,2048]{1,0:T(2,128)}, u32[]{:S(2)}) copy-start(f32[2,2048]{1,0:T(2,128)} %param.17) | copy-start | bytes 49156
  144.0 114.8 %all-to-all-start = ((bf16[32,2,2048]{2,1,0:T(2,128)(2,1)}), bf16[32,2,2048]{2,1,0:T(2,128)(2,1)S(1)}, u32[]{:S(2)}, u32[]{:S(2)}) async-start(bf16[32,2,2048]{2,1,0:T(2,128)(2,1)} %convert_element_type.228), calls=%async_computation | async-start | bytes 524288 | tf_op jit(solution)/shard_map/all_to_all | solution.py:107
  363.7 100.5 %copy-start.4 = (f32[2]{0:T(128)}, f32[2]{0:T(128)S(1)}, u32[]{:S(2)}) copy-start(f32[2]{0:T(128)S(1)} %div.15) | copy-start | bytes 28
  493.4 8.2 collective-permute-start.4
  496.2 9.3 collective-permute-start.5
  929.0 8.2 collective-permute-start.6
  931.7 9.3 collective-permute-start.7
  1016.2 218.3 %copy-start.2 = (f32[2,2048]{1,0:T(2,128)S(1)}, f32[2,2048]{1,0:T(2,128)}, u32[]{:S(2)}) copy-start(f32[2,2048]{1,0:T(2,128)} %param.17) | copy-start | bytes 49156
  1016.2 218.3 %copy-start.5 = (f32[2]{0:T(128)S(1)}, f32[2]{0:T(128)}, u32[]{:S(2)}) copy-start(f32[2]{0:T(128)} %copy-done.4) | copy-start | bytes 28
where the time goes:
time: 1250 us; the launch traced here: 1240 us
  blocking collectives  837 us (67%)
  matrix products  136 us (11%)
  starting transfers between devices  111 us (9%)
  loops' own time  70.6 us (6%)
  waiting for transfers between devices  53 us (4%)
  local copies, waits for them, and re-layouts  18.8 us (2%)
    all_to_all x2, blocking collectives, body(): lax.all_to_all(buffer.astype(jnp.bfloat16), 'tile', split_axis=0, concat_...  227 us
    psum x2, blocking collectives, body(): curvature = lax.psum(jnp.sum(direction * applied, axis=1), ('city', 'tile'))  209 us
    psum x2, blocking collectives, body(): norm_next = lax.psum(jnp.sum(residual * residual, axis=1), ('city', 'tile'))  201 us
    psum x1, blocking collectives, body(): norm_now = lax.psum(jnp.sum(residual * residual, axis=1), ('city', 'tile'))  104 us
    all_gather x3, blocking collectives, body(): city_dirs = lax.all_gather(own_dirs[None], 'tile', axis=0, tiled=True)  96 us
    all_to_all x1, starting transfers between devices, body(): lax.all_to_all(buffer.astype(jnp.bfloat16), 'tile', split_axis=0, concat_...  92.8 us
    dot_general x24, matrix products, compute(): lax.dot_general(far_vec, kernel, (((1,), (1,)), ((), ())), preferred_elem...  67.9 us
    dot_general x24, matrix products, compute(): jnp.dot(near_vec[:, offset:offset + row_block], kernel, preferred_element...  67.8 us
  transfers between devices with their start and end apart: 9, of which 8 were waited for; matrix products, arithmetic and copies ran while one was open for 0% of the time, Pallas kernels for 0%

commit v1 on v0

v1 whole, which is shorter than its diff:
```python
import jax
import jax.numpy as jnp
from jax import lax
from jax.experimental import pallas as pl
from jax.experimental.pallas import tpu as pltpu
from jax.sharding import PartitionSpec as P

SLOTS = 3
LANES = 128
SCALE = 4.0**0.2
HEAD = 5.0 / SCALE**4


def exchange_list(size, step):
    return [(i, i ^ step) for i in range(size)]


def tile_gather(block):
    size = lax.axis_size("tile")
    step = size // 2
    while step >= 1:
        other = lax.ppermute(block, "tile", exchange_list(size, step))
        block = jnp.concatenate([block, other], axis=0)
        step //= 2
    return block


def slot_of(tile):
    size = lax.axis_size("tile")
    bits = size.bit_length() - 1
    apart = jnp.bitwise_xor(tile, lax.axis_index("tile"))
    slot = jnp.zeros_like(apart)
    for bit in range(bits):
        slot = slot | (((apart >> bit) & 1) << (bits - 1 - bit))
    return slot


def axis_sum(values, axis):
    size = lax.axis_size(axis)
    step = 1
    while step < size:
        values = values + lax.ppermute(values, axis, exchange_list(size, step))
        step *= 2
    return values


def pick_tile(gathered, tile, length):
    picked = lax.dynamic_index_in_dim(gathered, slot_of(tile), 0, False)
    return picked[:, :length]


def city_moves():
    size = lax.axis_size("city")
    up = [(i, i + 1) for i in range(size - 1)]
    return up, [(j, i) for i, j in up]


def two_terms(values):
    high = values.astype(jnp.bfloat16).astype(jnp.float32)
    return jnp.concatenate([high, values - high], axis=0).astype(jnp.bfloat16)


def build_kernel(live, near_ref, far_ref, vec_ref, block_ref, out_ref):
    slot, part = pl.program_id(0), pl.program_id(1)
    rows, length = block_ref.shape[1:]
    width = min(1024, length)

    @pl.when((slot == 0) & (part == 0))
    def _():
        out_ref[...] = jnp.zeros_like(out_ref)

    @pl.when(live[slot] > 0)
    def _():
        far = jnp.transpose(far_ref[0])
        for top in range(0, rows, 16):
            far_x = far[top : top + 16, 0:1]
            far_y = far[top : top + 16, 1:2]
            for left in range(0, length, width):
                across = far_x - near_ref[0:1, left : left + width]
                along = far_y - near_ref[1:2, left : left + width]
                square = jnp.maximum(across * across + along * along, 1e-30)
                inside = jnp.maximum(SCALE - square * lax.rsqrt(square), 0.0)
                power = inside * inside
                value = power * power * (HEAD - inside)
                block_ref[0, top : top + 16, left : left + width] = value.astype(jnp.bfloat16)
        out_ref[...] += jnp.dot(
            two_terms(vec_ref[0]), block_ref[0], preferred_element_type=jnp.float32
        )


def apply_kernel(live, vec_ref, block_ref, out_ref):
    slot, part = pl.program_id(0), pl.program_id(1)

    @pl.when((slot == 0) & (part == 0))
    def _():
        out_ref[...] = jnp.zeros_like(out_ref)

    @pl.when(live[slot] > 0)
    def _():
        out_ref[...] += jnp.dot(
            two_terms(vec_ref[0]), block_ref[0], preferred_element_type=jnp.float32
        )


def eight_rows(values):
    return jnp.pad(values, ((0, 0), (0, 8 - values.shape[1]), (0, 0)))


def build(live, near, far, vecs):
    length = near.shape[1]
    rows = min(256, length)
    blocks, out = pl.pallas_call(
        build_kernel,
        grid_spec=pltpu.PrefetchScalarGridSpec(
            num_scalar_prefetch=1,
            grid=(SLOTS, length // rows),
            in_specs=[
                pl.BlockSpec((8, length), lambda s, p, live: (0, 0)),
                pl.BlockSpec((1, 8, rows), lambda s, p, live: (s, 0, p)),
                pl.BlockSpec((1, 8, rows), lambda s, p, live: (s, 0, p)),
            ],
            out_specs=[
                pl.BlockSpec((1, rows, length), lambda s, p, live: (s, p, 0)),
                pl.BlockSpec((16, length), lambda s, p, live: (0, 0)),
            ],
        ),
        out_shape=[
            jax.ShapeDtypeStruct((SLOTS, length, length), jnp.bfloat16),
            jax.ShapeDtypeStruct((16, length), jnp.float32),
        ],
        compiler_params=pltpu.CompilerParams(vmem_limit_bytes=32 * 1024 * 1024),
        cost_estimate=pl.CostEstimate(
            flops=SLOTS * length * length * 16,
            bytes_accessed=SLOTS * length * length * 2,
            transcendentals=SLOTS * length * length,
        ),
        name="build",
    )(live, jnp.pad(near, ((0, 6), (0, 0))), eight_rows(far), eight_rows(vecs))
    return blocks, out[0:2] + out[8:10]


def apply(live, vecs, blocks):
    length = vecs.shape[2]
    rows = min(256, length)
    out = pl.pallas_call(
        apply_kernel,
        grid_spec=pltpu.PrefetchScalarGridSpec(
            num_scalar_prefetch=1,
            grid=(SLOTS, length // rows),
            in_specs=[
                pl.BlockSpec((1, 8, rows), lambda s, p, live: (s, 0, p)),
                pl.BlockSpec((1, rows, length), lambda s, p, live: (s, p, 0)),
            ],
            out_specs=pl.BlockSpec((16, length), lambda s, p, live: (0, 0)),
        ),
        out_shape=jax.ShapeDtypeStruct((16, length), jnp.float32),
        compiler_params=pltpu.CompilerParams(vmem_limit_bytes=32 * 1024 * 1024),
        cost_estimate=pl.CostEstimate(
            flops=SLOTS * length * length * 16,
            bytes_accessed=SLOTS * length * length * 2,
            transcendentals=0,
        ),
        name="apply",
    )(live, eight_rows(vecs), blocks)
    return out[0:2] + out[8:10]


def dots(pairs):
    sums = [jnp.sum(a * b, axis=1) for a, b in pairs]
    return jnp.pad(jnp.stack(sums, axis=1), ((0, 0), (0, LANES - len(sums))))


def body(right_side, noise_var, coords, counts, pair_list):
    own = lax.axis_index("tile")
    size = lax.axis_size("tile")
    length = right_side.shape[1]
    up, down = city_moves()
    valid_mask = (jnp.arange(length) < counts[0]).astype(jnp.float32)
    noise_eff = jnp.where(valid_mask > 0, noise_var, 1.0)
    res_0 = right_side * valid_mask[None, :]

    table = pair_list.reshape(1, -1).astype(jnp.float32)
    entries = table.shape[1]
    table = jnp.pad(table, ((0, 1), (0, LANES - entries)))
    gathered = tile_gather(jnp.concatenate([res_0, table], axis=1)[None])
    rows = gathered[:, 0, length : length + entries].reshape(-1, 3).astype(jnp.int32)
    first, second, kind = rows[:, 0], rows[:, 1], rows[:, 2]

    shift = jnp.where(kind == 2, size, jnp.where(kind == 3, 2 * size, 0))
    code_near = jnp.where((kind > 0) & (first == own), second + shift, -1)
    code_far = jnp.where((kind == 1) & (first != second) & (second == own), first, -1)
    codes = jnp.concatenate([code_near, code_far])
    code = [jnp.max(codes)]
    for _ in range(SLOTS - 1):
        code.append(jnp.max(jnp.where(codes < code[-1], codes, -1)))
    live = jnp.stack([(c >= 0).astype(jnp.int32) for c in code])
    up_tile = jnp.maximum(jnp.max(jnp.where(kind == 2, first, -1)), 0)
    down_tile = jnp.maximum(jnp.max(jnp.where(kind == 3, first, -1)), 0)

    def coords_of(tile):
        return lax.dynamic_slice_in_dim(coords, tile * length, length, 1)

    def select(here, from_next, from_prev, number):
        return jnp.where(number < size, here, jnp.where(number < 2 * size, from_next, from_prev))

    def partners(gathered, extra_of=None):
        ups = pick_tile(gathered, up_tile, length)
        downs = pick_tile(gathered, down_tile, length)
        if extra_of is not None:
            ups = jnp.concatenate([ups, extra_of(up_tile)])
            downs = jnp.concatenate([downs, extra_of(down_tile)])
        from_prev = lax.ppermute(ups, "city", up)
        from_next = lax.ppermute(downs, "city", down)
        chosen = []
        for number in code:
            tile = jnp.bitwise_and(jnp.maximum(number, 0), size - 1)
            here = pick_tile(gathered, tile, length)
            if extra_of is not None:
                here = jnp.concatenate([here, extra_of(tile)])
            chosen.append(select(here, from_next, from_prev, number))
        return jnp.stack(chosen)

    def whole(summed, vec):
        return valid_mask[None, :] * summed + noise_eff[None, :] * vec

    chosen = partners(gathered, coords_of)
    near = coords_of(own)
    origin = near[:, 0:1]
    blocks, summed = build(
        live, (near - origin) * SCALE, (chosen[:, 2:4] - origin) * SCALE, chosen[:, 0:2]
    )
    img_0 = whole(summed, res_0)

    def exchange(vec, pairs):
        gathered = tile_gather(jnp.concatenate([vec, dots(pairs)], axis=1)[None])
        part = jnp.sum(gathered[:, :, length:], axis=0)
        totals = axis_sum(part, "city")[:, 0 : len(pairs)]
        return whole(apply(live, partners(gathered), blocks), vec), totals

    img_img_0, totals = exchange(img_0, [(res_0, res_0), (res_0, img_0), (img_0, img_0)])
    rr_0, curve_0, square_0 = totals[:, 0:1], totals[:, 1:2], totals[:, 2:3]
    step_1 = rr_0 / curve_0
    rr_1 = jnp.maximum(rr_0 - 2.0 * step_1 * curve_0 + step_1 * step_1 * square_0, 0.0)
    beta_1 = rr_1 / rr_0
    res_1 = res_0 - step_1 * img_0
    img_1 = img_0 - step_1 * img_img_0
    dir_1 = res_1 + beta_1 * res_0
    dir_img_1 = img_1 + beta_1 * img_0

    img_img_1, totals = exchange(
        img_1,
        [(res_1, res_1), (dir_1, dir_img_1), (res_1, dir_img_1), (dir_img_1, dir_img_1)],
    )
    rr_1, curve_1 = totals[:, 0:1], totals[:, 1:2]
    step_2 = rr_1 / curve_1
    rr_2 = rr_1 - 2.0 * step_2 * totals[:, 2:3] + step_2 * step_2 * totals[:, 3:4]
    beta_2 = jnp.maximum(rr_2, 0.0) / rr_1
    res_2 = res_1 - step_2 * dir_img_1
    img_2 = img_1 - step_2 * (img_img_1 + beta_1 * img_img_0)
    dir_2 = res_2 + beta_2 * dir_1
    dir_img_2 = img_2 + beta_2 * dir_img_1
    field_2 = step_1 * res_0 + step_2 * dir_1

    last = axis_sum(axis_sum(dots([(res_2, res_2), (dir_2, dir_img_2)]), "tile"), "city")
    step_3 = last[:, 0:1] / last[:, 1:2]
    return (field_2 + step_3 * dir_2, res_2 - step_3 * dir_img_2)


def solution(mesh):
    placed = (
        P(None, ("city", "tile")),
        P(("city", "tile")),
        P(None, "city"),
        P(("city", "tile")),
        P(("city", "tile"), None, None),
    )
    return jax.shard_map(
        body,
        mesh=mesh,
        in_specs=placed,
        out_specs=(P(None, ("city", "tile")), P(None, ("city", "tile"))),
        check_vma=False,
    )
```

time: 1250 us -> 372 us (0.30)
  the two profiles are of different devices: /device:TPU:1 before, /device:TPU:6 now
where the time goes in v1:
time: 372 us; the launch traced here: 370 us
  starting transfers between devices  146 us (39%)
  waiting for transfers between devices  129 us (35%)
  Pallas kernels  72.5 us (19%)
  between operations  9.76 us (3%)
  other arithmetic  9.29 us (2%)
    ppermute x15, starting transfers between devices, tile_gather(): other = lax.ppermute(block, 'tile', exchange_list(size, step))  75.1 us
    ppermute x17, waiting for transfers between devices, axis_sum(): values = values + lax.ppermute(values, axis, exchange_list(size, step))  65.4 us
    ppermute x15, waiting for transfers between devices, tile_gather(): other = lax.ppermute(block, 'tile', exchange_list(size, step))  52.9 us
    ppermute x17, starting transfers between devices, axis_sum(): values = values + lax.ppermute(values, axis, exchange_list(size, step))  51.7 us
    pallas_call x2, Pallas kernels, apply(): pl.pallas_call(apply_kernel, grid_spec=pltpu.PrefetchScalarGridSpec(num_s...  38.9 us
    pallas_call x1, Pallas kernels, build(): pl.pallas_call(build_kernel, grid_spec=pltpu.PrefetchScalarGridSpec(num_s...  33.6 us
    ppermute x3, waiting for transfers between devices, partners(): from_prev = lax.ppermute(ups, 'city', up)  11.2 us
    ppermute x3, starting transfers between devices, partners(): from_next = lax.ppermute(downs, 'city', down)  9.75 us
  transfers between devices with their start and end apart: 38, of which 32 were waited for; matrix products, arithmetic and copies ran while one was open for 1% of the time, Pallas kernels for 0%

profile of v1, /device:TPU:6, one launch (start us, length us, event | category | flops | bytes accessed | tf_op | source)
XLA Modules:
  0.0 369.6 jit_solution(18316412508869805395)
XLA Ops:
  2.9 15.7 %collective-permute-start = (f32[1,2,2176]{2,1,0:T(2,128)S(1)}, f32[1,2,2176]{2,1,0:T(2,128)S(1)}, u32[]{:S(2)}, u32[]{:S(2)}) collective-permute-start(f32[1,2,2176]{2,1,0:T(2,128)S(1)} %fusion.5), channel_id=1, source_target_pairs={{0,16},{1,17},{2,18},{3,19},{4,20},{5,21},{6,22},{7,23},{8,24},{9,... | collective-permute-start | bytes 52232 | tf_op jit(solution)/shard_map/ppermute | solution.py:22
  20.4 6.0 %collective-permute-start.1 = (f32[2,2,2176]{2,1,0:T(2,128)S(1)}, f32[2,2,2176]{2,1,0:T(2,128)S(1)}, u32[]{:S(2)}, u32[]{:S(2)}) collective-permute-start(f32[2,2,2176]{2,1,0:T(2,128)S(1)} %pad_maximum_fusion.7), channel_id=1, source_target_pairs={{0,8},{1,9},{2,10},{3,11},{4,12},{5,13},{6,14},{7,15},{8,0},{9,1},... | collective-permute-start | bytes 104456 | tf_op jit(solution)/shard_map/ppermute | solution.py:22
  33.9 4.5 %collective-permute-done.2 = f32[4,2,2176]{2,1,0:T(2,128)S(1)} collective-permute-done((f32[4,2,2176]{2,1,0:T(2,128)S(1)}, f32[4,2,2176]{2,1,0:T(2,128)S(1)}, u32[]{:S(2)}, u32[]{:S(2)}) %collective-permute-start.2) | collective-permute-done | bytes 69664 | tf_op jit(solution)/shard_map/ppermute | solution.py:22
  40.7 4.7 %collective-permute-done.3 = f32[8,2,2176]{2,1,0:T(2,128)S(1)} collective-permute-done((f32[8,2,2176]{2,1,0:T(2,128)S(1)}, f32[8,2,2176]{2,1,0:T(2,128)S(1)}, u32[]{:S(2)}, u32[]{:S(2)}) %collective-permute-start.3) | collective-permute-done | bytes 139296 | tf_op jit(solution)/shard_map/ppermute | solution.py:22
  58.8 5.2 %collective-permute-start.5 = (f32[4,2048]{1,0:T(4,128)S(1)}, f32[4,2048]{1,0:T(4,128)S(1)}, u32[]{:S(2)}, u32[]{:S(2)}) collective-permute-start(f32[4,2048]{1,0:T(4,128)S(1)} %pad_maximum_fusion.10), channel_id=1, source_target_pairs={{32,0},{64,32},{96,64},{128,96},{160,128},{192,160},{224,192},{256... | collective-permute-start | bytes 98312 | tf_op jit(solution)/shard_map/ppermute | solution.py:213
  72.2 33.6 %build.1 = (bf16[3,2048,2048]{2,1,0:T(8,128)(2,1)}, f32[16,2048]{1,0:T(8,128)S(1)}) custom-call(s32[3]{0:T(128)S(1)} %add_convert_fusion.live, f32[8,2048]{1,0:T(8,128)S(1)} %pad.34.near_ref, f32[3,8,2048]{2,1,0:T(8,128)S(1)} %pad.35.far_ref, f32[3,8,2048]{2,1,0:T(8,128)S(1)} %pad.36.vec_ref), custom_call_target="tpu_custom_call" | custom-call | flops 201326592 | bytes 25165824 | tf_op jit(solution)/shard_map/build/pallas_call | solution.py:112
  106.4 12.3 %collective-permute-start.7 = (f32[1,2,2176]{2,1,0:T(2,128)S(1)}, f32[1,2,2176]{2,1,0:T(2,128)S(1)}, u32[]{:S(2)}, u32[]{:S(2)}) collective-permute-start(f32[1,2,2176]{2,1,0:T(2,128)S(1)} %maximum_bitcast_fusion), channel_id=1, source_target_pairs={{0,16},{1,17},{2,18},{3,19},{4,20},{5,21},{6,22},{7,23},{8,24},{9,... | collective-permute-start | bytes 52232 | tf_op jit(solution)/shard_map/ppermute | solution.py:22
  120.8 5.3 %collective-permute-start.8 = (f32[2,2,2176]{2,1,0:T(2,128)S(1)}, f32[2,2,2176]{2,1,0:T(2,128)S(1)}, u32[]{:S(2)}, u32[]{:S(2)}) collective-permute-start(f32[2,2,2176]{2,1,0:T(2,128)S(1)} %pad_maximum_fusion.8), channel_id=1, source_target_pairs={{0,8},{1,9},{2,10},{3,11},{4,12},{5,13},{6,14},{7,15},{8,0},{9,1},... | collective-permute-start | bytes 104456 | tf_op jit(solution)/shard_map/ppermute | solution.py:22
  126.1 4.9 %collective-permute-done.8 = f32[2,2,2176]{2,1,0:T(2,128)S(1)} collective-permute-done((f32[2,2,2176]{2,1,0:T(2,128)S(1)}, f32[2,2,2176]{2,1,0:T(2,128)S(1)}, u32[]{:S(2)}, u32[]{:S(2)}) %collective-permute-start.8) | collective-permute-done | bytes 34848 | tf_op jit(solution)/shard_map/ppermute | solution.py:22
  133.3 4.8 %collective-permute-done.9 = f32[4,2,2176]{2,1,0:T(2,128)S(1)} collective-permute-done((f32[4,2,2176]{2,1,0:T(2,128)S(1)}, f32[4,2,2176]{2,1,0:T(2,128)S(1)}, u32[]{:S(2)}, u32[]{:S(2)}) %collective-permute-start.9) | collective-permute-done | bytes 69664 | tf_op jit(solution)/shard_map/ppermute | solution.py:22
  140.2 5.0 %collective-permute-done.10 = f32[8,2,2176]{2,1,0:T(2,128)S(1)} collective-permute-done((f32[8,2,2176]{2,1,0:T(2,128)S(1)}, f32[8,2,2176]{2,1,0:T(2,128)S(1)}, u32[]{:S(2)}, u32[]{:S(2)}) %collective-permute-start.10) | collective-permute-done | bytes 139296 | tf_op jit(solution)/shard_map/ppermute | solution.py:22
  156.2 5.0 %collective-permute-done.13 = f32[2,128]{1,0:T(2,128)S(1)} collective-permute-done((f32[2,128]{1,0:T(2,128)S(1)}, f32[2,128]{1,0:T(2,128)S(1)}, u32[]{:S(2)}, u32[]{:S(2)}) %collective-permute-start.13) | collective-permute-done | bytes 1056 | tf_op jit(solution)/shard_map/ppermute | solution.py:42
  175.9 4.3 %collective-permute-done.17 = f32[2,2048]{1,0:T(2,128)S(1)} collective-permute-done((f32[2,2048]{1,0:T(2,128)S(1)}, f32[2,2048]{1,0:T(2,128)S(1)}, u32[]{:S(2)}, u32[]{:S(2)}) %collective-permute-start.17) | collective-permute-done | bytes 16416 | tf_op jit(solution)/shard_map/ppermute | solution.py:212
  180.2 19.5 %apply.2 = f32[16,2048]{1,0:T(8,128)S(1)} custom-call(s32[3]{0:T(128)S(1)} %add_convert_fusion.live, f32[3,8,2048]{2,1,0:T(8,128)S(1)} %select_maximum_fusion.2.vec_ref, bf16[3,2048,2048]{2,1,0:T(8,128)(2,1)} %get-tuple-element.5.block_ref), custom_call_target="tpu_custom_call" | custom-call | flops 201326592 | bytes 25165824 | tf_op jit(solution)/shard_map/apply/pallas_call | solution.py:145
  200.4 12.0 %collective-permute-start.18 = (f32[1,2,2176]{2,1,0:T(2,128)S(1)}, f32[1,2,2176]{2,1,0:T(2,128)S(1)}, u32[]{:S(2)}, u32[]{:S(2)}) collective-permute-start(f32[1,2,2176]{2,1,0:T(2,128)S(1)} %maximum_bitcast_fusion.1), channel_id=1, source_target_pairs={{0,16},{1,17},{2,18},{3,19},{4,20},{5,21},{6,22},{7,23},{8,24},{9,... | collective-permute-start | bytes 52232 | tf_op jit(solution)/shard_map/ppermute | solution.py:22
  214.8 4.5 %collective-permute-start.19 = (f32[2,2,2176]{2,1,0:T(2,128)S(1)}, f32[2,2,2176]{2,1,0:T(2,128)S(1)}, u32[]{:S(2)}, u32[]{:S(2)}) collective-permute-start(f32[2,2,2176]{2,1,0:T(2,128)S(1)} %pad_maximum_fusion.9), channel_id=1, source_target_pairs={{0,8},{1,9},{2,10},{3,11},{4,12},{5,13},{6,14},{7,15},{8,0},{9,1},... | collective-permute-start | bytes 104456 | tf_op jit(solution)/shard_map/ppermute | solution.py:22
  219.3 5.4 %collective-permute-done.19 = f32[2,2,2176]{2,1,0:T(2,128)S(1)} collective-permute-done((f32[2,2,2176]{2,1,0:T(2,128)S(1)}, f32[2,2,2176]{2,1,0:T(2,128)S(1)}, u32[]{:S(2)}, u32[]{:S(2)}) %collective-permute-start.19) | collective-permute-done | bytes 34848 | tf_op jit(solution)/shard_map/ppermute | solution.py:22
  226.7 5.5 %collective-permute-done.20 = f32[4,2,2176]{2,1,0:T(2,128)S(1)} collective-permute-done((f32[4,2,2176]{2,1,0:T(2,128)S(1)}, f32[4,2,2176]{2,1,0:T(2,128)S(1)}, u32[]{:S(2)}, u32[]{:S(2)}) %collective-permute-start.20) | collective-permute-done | bytes 69664 | tf_op jit(solution)/shard_map/ppermute | solution.py:22
  234.3 5.0 %collective-permute-done.21 = f32[8,2,2176]{2,1,0:T(2,128)S(1)} collective-permute-done((f32[8,2,2176]{2,1,0:T(2,128)S(1)}, f32[8,2,2176]{2,1,0:T(2,128)S(1)}, u32[]{:S(2)}, u32[]{:S(2)}) %collective-permute-start.21) | collective-permute-done | bytes 139296 | tf_op jit(solution)/shard_map/ppermute | solution.py:22
  250.2 5.0 %collective-permute-done.24 = f32[2,128]{1,0:T(2,128)S(1)} collective-permute-done((f32[2,128]{1,0:T(2,128)S(1)}, f32[2,128]{1,0:T(2,128)S(1)}, u32[]{:S(2)}, u32[]{:S(2)}) %collective-permute-start.24) | collective-permute-done | bytes 1056 | tf_op jit(solution)/shard_map/ppermute | solution.py:42
  260.7 5.5 %collective-permute-start.26 = (f32[2,128]{1,0:T(2,128)S(1)}, f32[2,128]{1,0:T(2,128)S(1)}, u32[]{:S(2)}, u32[]{:S(2)}) collective-permute-start(f32[2,128]{1,0:T(2,128)S(1)} %add.186), channel_id=1, source_target_pairs={{0,256},{32,288},{64,320},{96,352},{128,384},{160,416},{192,448},{... | collective-permute-start | bytes 3080 | tf_op jit(solution)/shard_map/ppermute | solution.py:42
  276.1 19.5 %apply.3 = f32[16,2048]{1,0:T(8,128)S(1)} custom-call(s32[3]{0:T(128)S(1)} %add_convert_fusion.live, f32[3,8,2048]{2,1,0:T(8,128)S(1)} %select_maximum_fusion.vec_ref, bf16[3,2048,2048]{2,1,0:T(8,128)(2,1)} %get-tuple-element.5.block_ref), custom_call_target="tpu_custom_call" | custom-call | flops 201326592 | bytes 25165824 | tf_op jit(solution)/shard_map/apply/pallas_call | solution.py:145
  300.9 4.2 %collective-permute-done.30 = f32[2,128]{0,1:T(8,128)S(1)} collective-permute-done((f32[2,128]{0,1:T(8,128)S(1)}, f32[2,128]{0,1:T(8,128)S(1)}, u32[]{:S(2)}, u32[]{:S(2)}) %collective-permute-start.30) | collective-permute-done | bytes 1056 | tf_op jit(solution)/shard_map/ppermute | solution.py:42
  307.2 5.3 %collective-permute-done.31 = f32[2,128]{0,1:T(8,128)S(1)} collective-permute-done((f32[2,128]{0,1:T(8,128)S(1)}, f32[2,128]{0,1:T(8,128)S(1)}, u32[]{:S(2)}, u32[]{:S(2)}) %collective-permute-start.31) | collective-permute-done | bytes 1056 | tf_op jit(solution)/shard_map/ppermute | solution.py:42
  312.5 5.4 %collective-permute-start.32 = (f32[2,128]{0,1:T(8,128)S(1)}, f32[2,128]{0,1:T(8,128)S(1)}, u32[]{:S(2)}, u32[]{:S(2)}) collective-permute-start(f32[2,128]{0,1:T(8,128)S(1)} %add.197), channel_id=1, source_target_pairs={{0,8},{1,9},{2,10},{3,11},{4,12},{5,13},{6,14},{7,15},{8,0},{9,1},... | collective-permute-start | bytes 3080 | tf_op jit(solution)/shard_map/ppermute | solution.py:42
  317.9 6.5 %collective-permute-done.32 = f32[2,128]{0,1:T(8,128)S(1)} collective-permute-done((f32[2,128]{0,1:T(8,128)S(1)}, f32[2,128]{0,1:T(8,128)S(1)}, u32[]{:S(2)}, u32[]{:S(2)}) %collective-permute-start.32) | collective-permute-done | bytes 1056 | tf_op jit(solution)/shard_map/ppermute | solution.py:42
  324.4 11.1 %collective-permute-start.33 = (f32[2,128]{0,1:T(8,128)S(1)}, f32[2,128]{0,1:T(8,128)S(1)}, u32[]{:S(2)}, u32[]{:S(2)}) collective-permute-start(f32[2,128]{0,1:T(8,128)S(1)} %add.198), channel_id=1, source_target_pairs={{0,16},{1,17},{2,18},{3,19},{4,20},{5,21},{6,22},{7,23},{8,24},{9,... | collective-permute-start | bytes 3080 | tf_op jit(solution)/shard_map/ppermute | solution.py:42
  335.5 5.1 %collective-permute-done.33 = f32[2,128]{0,1:T(8,128)S(1)} collective-permute-done((f32[2,128]{0,1:T(8,128)S(1)}, f32[2,128]{0,1:T(8,128)S(1)}, u32[]{:S(2)}, u32[]{:S(2)}) %collective-permute-start.33) | collective-permute-done | bytes 1056 | tf_op jit(solution)/shard_map/ppermute | solution.py:42
  342.6 4.7 %collective-permute-done.34 = f32[2,128]{0,1:T(8,128)S(1)} collective-permute-done((f32[2,128]{0,1:T(8,128)S(1)}, f32[2,128]{0,1:T(8,128)S(1)}, u32[]{:S(2)}, u32[]{:S(2)}) %collective-permute-start.34) | collective-permute-done | bytes 1056 | tf_op jit(solution)/shard_map/ppermute | solution.py:42
  349.2 5.7 %collective-permute-done.35 = f32[2,128]{0,1:T(8,128)S(1)} collective-permute-done((f32[2,128]{0,1:T(8,128)S(1)}, f32[2,128]{0,1:T(8,128)S(1)}, u32[]{:S(2)}, u32[]{:S(2)}) %collective-permute-start.35) | collective-permute-done | bytes 1056 | tf_op jit(solution)/shard_map/ppermute | solution.py:42
  356.9 4.2 %collective-permute-done.36 = f32[2,128]{0,1:T(8,128)S(1)} collective-permute-done((f32[2,128]{0,1:T(8,128)S(1)}, f32[2,128]{0,1:T(8,128)S(1)}, u32[]{:S(2)}, u32[]{:S(2)}) %collective-permute-start.36) | collective-permute-done | bytes 1056 | tf_op jit(solution)/shard_map/ppermute | solution.py:42
  363.1 5.7 %collective-permute-done.37 = f32[2,128]{0,1:T(8,128)S(1)} collective-permute-done((f32[2,128]{0,1:T(8,128)S(1)}, f32[2,128]{0,1:T(8,128)S(1)}, u32[]{:S(2)}, u32[]{:S(2)}) %collective-permute-start.37) | collective-permute-done | bytes 1056 | tf_op jit(solution)/shard_map/ppermute | solution.py:42
  (155 shorter events, 108.6 us)
Async XLA Ops:
  2.9 17.4 %collective-permute-start = (f32[1,2,2176]{2,1,0:T(2,128)S(1)}, f32[1,2,2176]{2,1,0:T(2,128)S(1)}, u32[]{:S(2)}, u32[]{:S(2)}) collective-permute-start(f32[1,2,2176]{2,1,0:T(2,128)S(1)} %fusion.5), channel_id=1, source_target_pairs={{0,16},{1,17},{2,18},{3,19},{4,20},{5,21},{6,22},{7,23},{8,24},{9,... | collective-permute-start | bytes 52232 | tf_op jit(solution)/shard_map/ppermute | solution.py:22
  20.4 10.1 %collective-permute-start.1 = (f32[2,2,2176]{2,1,0:T(2,128)S(1)}, f32[2,2,2176]{2,1,0:T(2,128)S(1)}, u32[]{:S(2)}, u32[]{:S(2)}) collective-permute-start(f32[2,2,2176]{2,1,0:T(2,128)S(1)} %pad_maximum_fusion.7), channel_id=1, source_target_pairs={{0,8},{1,9},{2,10},{3,11},{4,12},{5,13},{6,14},{7,15},{8,0},{9,1},... | collective-permute-start | bytes 104456 | tf_op jit(solution)/shard_map/ppermute | solution.py:22
  30.5 7.8 %collective-permute-start.2 = (f32[4,2,2176]{2,1,0:T(2,128)S(1)}, f32[4,2,2176]{2,1,0:T(2,128)S(1)}, u32[]{:S(2)}, u32[]{:S(2)}) collective-permute-start(f32[4,2,2176]{2,1,0:T(2,128)S(1)} %pad_maximum_fusion.4), channel_id=1, source_target_pairs={{0,4},{1,5},{2,6},{3,7},{4,0},{5,1},{6,2},{7,3},{8,12},{9,13},{10,... | collective-permute-start | bytes 208904 | tf_op jit(solution)/shard_map/ppermute | solution.py:22
  38.4 6.9 %collective-permute-start.3 = (f32[8,2,2176]{2,1,0:T(2,128)S(1)}, f32[8,2,2176]{2,1,0:T(2,128)S(1)}, u32[]{:S(2)}, u32[]{:S(2)}) collective-permute-start(f32[8,2,2176]{2,1,0:T(2,128)S(1)} %pad_maximum_fusion), channel_id=1, source_target_pairs={{0,2},{1,3},{2,0},{3,1},{4,6},{5,7},{6,4},{7,5},{8,10},{9,11},{10,... | collective-permute-start | bytes 417800 | tf_op jit(solution)/shard_map/ppermute | solution.py:22
  58.8 9.8 %collective-permute-start.5 = (f32[4,2048]{1,0:T(4,128)S(1)}, f32[4,2048]{1,0:T(4,128)S(1)}, u32[]{:S(2)}, u32[]{:S(2)}) collective-permute-start(f32[4,2048]{1,0:T(4,128)S(1)} %pad_maximum_fusion.10), channel_id=1, source_target_pairs={{32,0},{64,32},{96,64},{128,96},{160,128},{192,160},{224,192},{256... | collective-permute-start | bytes 98312 | tf_op jit(solution)/shard_map/ppermute | solution.py:213
  64.1 7.9 %collective-permute-start.6 = (f32[4,2048]{1,0:T(4,128)S(1)}, f32[4,2048]{1,0:T(4,128)S(1)}, u32[]{:S(2)}, u32[]{:S(2)}) collective-permute-start(f32[4,2048]{1,0:T(4,128)S(1)} %pad_maximum_fusion.11), channel_id=1, source_target_pairs={{0,32},{32,64},{64,96},{96,128},{128,160},{160,192},{192,224},{224... | collective-permute-start | bytes 98312 | tf_op jit(solution)/shard_map/ppermute | solution.py:212
  106.4 14.4 %collective-permute-start.7 = (f32[1,2,2176]{2,1,0:T(2,128)S(1)}, f32[1,2,2176]{2,1,0:T(2,128)S(1)}, u32[]{:S(2)}, u32[]{:S(2)}) collective-permute-start(f32[1,2,2176]{2,1,0:T(2,128)S(1)} %maximum_bitcast_fusion), channel_id=1, source_target_pairs={{0,16},{1,17},{2,18},{3,19},{4,20},{5,21},{6,22},{7,23},{8,24},{9,... | collective-permute-start | bytes 52232 | tf_op jit(solution)/shard_map/ppermute | solution.py:22
  120.8 10.2 %collective-permute-start.8 = (f32[2,2,2176]{2,1,0:T(2,128)S(1)}, f32[2,2,2176]{2,1,0:T(2,128)S(1)}, u32[]{:S(2)}, u32[]{:S(2)}) collective-permute-start(f32[2,2,2176]{2,1,0:T(2,128)S(1)} %pad_maximum_fusion.8), channel_id=1, source_target_pairs={{0,8},{1,9},{2,10},{3,11},{4,12},{5,13},{6,14},{7,15},{8,0},{9,1},... | collective-permute-start | bytes 104456 | tf_op jit(solution)/shard_map/ppermute | solution.py:22
  131.0 7.1 %collective-permute-start.9 = (f32[4,2,2176]{2,1,0:T(2,128)S(1)}, f32[4,2,2176]{2,1,0:T(2,128)S(1)}, u32[]{:S(2)}, u32[]{:S(2)}) collective-permute-start(f32[4,2,2176]{2,1,0:T(2,128)S(1)} %pad_maximum_fusion.5), channel_id=1, source_target_pairs={{0,4},{1,5},{2,6},{3,7},{4,0},{5,1},{6,2},{7,3},{8,12},{9,13},{10,... | collective-permute-start | bytes 208904 | tf_op jit(solution)/shard_map/ppermute | solution.py:22
  138.2 6.9 %collective-permute-start.10 = (f32[8,2,2176]{2,1,0:T(2,128)S(1)}, f32[8,2,2176]{2,1,0:T(2,128)S(1)}, u32[]{:S(2)}, u32[]{:S(2)}) collective-permute-start(f32[8,2,2176]{2,1,0:T(2,128)S(1)} %pad_maximum_fusion.1), channel_id=1, source_target_pairs={{0,2},{1,3},{2,0},{3,1},{4,6},{5,7},{6,4},{7,5},{8,10},{9,11},{10,... | collective-permute-start | bytes 417800 | tf_op jit(solution)/shard_map/ppermute | solution.py:22
  148.8 5.5 %collective-permute-start.12 = (f32[2,128]{1,0:T(2,128)S(1)}, f32[2,128]{1,0:T(2,128)S(1)}, u32[]{:S(2)}, u32[]{:S(2)}) collective-permute-start(f32[2,128]{1,0:T(2,128)S(1)} %slice_reduce_fusion.3), channel_id=1, source_target_pairs={{0,32},{32,0},{64,96},{96,64},{128,160},{160,128},{192,224},{224,1... | collective-permute-start | bytes 3080 | tf_op jit(solution)/shard_map/ppermute | solution.py:42
  154.3 7.0 %collective-permute-start.13 = (f32[2,128]{1,0:T(2,128)S(1)}, f32[2,128]{1,0:T(2,128)S(1)}, u32[]{:S(2)}, u32[]{:S(2)}) collective-permute-start(f32[2,128]{1,0:T(2,128)S(1)} %add.175), channel_id=1, source_target_pairs={{0,64},{32,96},{64,0},{96,32},{128,192},{160,224},{192,128},{224,1... | collective-permute-start | bytes 3080 | tf_op jit(solution)/shard_map/ppermute | solution.py:42
  166.7 8.9 %collective-permute-start.15 = (f32[2,128]{1,0:T(2,128)S(1)}, f32[2,128]{1,0:T(2,128)S(1)}, u32[]{:S(2)}, u32[]{:S(2)}) collective-permute-start(f32[2,128]{1,0:T(2,128)S(1)} %add.177), channel_id=1, source_target_pairs={{0,256},{32,288},{64,320},{96,352},{128,384},{160,416},{192,448},{... | collective-permute-start | bytes 3080 | tf_op jit(solution)/shard_map/ppermute | solution.py:42
  169.7 6.1 %collective-permute-start.16 = (f32[2,2048]{1,0:T(2,128)S(1)}, f32[2,2048]{1,0:T(2,128)S(1)}, u32[]{:S(2)}, u32[]{:S(2)}) collective-permute-start(f32[2,2048]{1,0:T(2,128)S(1)} %slice.178), channel_id=1, source_target_pairs={{32,0},{64,32},{96,64},{128,96},{160,128},{192,160},{224,192},{256... | collective-permute-start | bytes 49160 | tf_op jit(solution)/shard_map/ppermute | solution.py:213
  172.4 7.7 %collective-permute-start.17 = (f32[2,2048]{1,0:T(2,128)S(1)}, f32[2,2048]{1,0:T(2,128)S(1)}, u32[]{:S(2)}, u32[]{:S(2)}) collective-permute-start(f32[2,2048]{1,0:T(2,128)S(1)} %slice.179), channel_id=1, source_target_pairs={{0,32},{32,64},{64,96},{96,128},{128,160},{160,192},{192,224},{224... | collective-permute-start | bytes 49160 | tf_op jit(solution)/shard_map/ppermute | solution.py:212
  200.4 14.4 %collective-permute-start.18 = (f32[1,2,2176]{2,1,0:T(2,128)S(1)}, f32[1,2,2176]{2,1,0:T(2,128)S(1)}, u32[]{:S(2)}, u32[]{:S(2)}) collective-permute-start(f32[1,2,2176]{2,1,0:T(2,128)S(1)} %maximum_bitcast_fusion.1), channel_id=1, source_target_pairs={{0,16},{1,17},{2,18},{3,19},{4,20},{5,21},{6,22},{7,23},{8,24},{9,... | collective-permute-start | bytes 52232 | tf_op jit(solution)/shard_map/ppermute | solution.py:22
  214.8 9.9 %collective-permute-start.19 = (f32[2,2,2176]{2,1,0:T(2,128)S(1)}, f32[2,2,2176]{2,1,0:T(2,128)S(1)}, u32[]{:S(2)}, u32[]{:S(2)}) collective-permute-start(f32[2,2,2176]{2,1,0:T(2,128)S(1)} %pad_maximum_fusion.9), channel_id=1, source_target_pairs={{0,8},{1,9},{2,10},{3,11},{4,12},{5,13},{6,14},{7,15},{8,0},{9,1},... | collective-permute-start | bytes 104456 | tf_op jit(solution)/shard_map/ppermute | solution.py:22
  224.7 7.5 %collective-permute-start.20 = (f32[4,2,2176]{2,1,0:T(2,128)S(1)}, f32[4,2,2176]{2,1,0:T(2,128)S(1)}, u32[]{:S(2)}, u32[]{:S(2)}) collective-permute-start(f32[4,2,2176]{2,1,0:T(2,128)S(1)} %pad_maximum_fusion.6), channel_id=1, source_target_pairs={{0,4},{1,5},{2,6},{3,7},{4,0},{5,1},{6,2},{7,3},{8,12},{9,13},{10,... | collective-permute-start | bytes 208904 | tf_op jit(solution)/shard_map/ppermute | solution.py:22
  232.3 6.9 %collective-permute-start.21 = (f32[8,2,2176]{2,1,0:T(2,128)S(1)}, f32[8,2,2176]{2,1,0:T(2,128)S(1)}, u32[]{:S(2)}, u32[]{:S(2)}) collective-permute-start(f32[8,2,2176]{2,1,0:T(2,128)S(1)} %pad_maximum_fusion.2), channel_id=1, source_target_pairs={{0,2},{1,3},{2,0},{3,1},{4,6},{5,7},{6,4},{7,5},{8,10},{9,11},{10,... | collective-permute-start | bytes 417800 | tf_op jit(solution)/shard_map/ppermute | solution.py:22
  242.9 5.5 %collective-permute-start.23 = (f32[2,128]{1,0:T(2,128)S(1)}, f32[2,128]{1,0:T(2,128)S(1)}, u32[]{:S(2)}, u32[]{:S(2)}) collective-permute-start(f32[2,128]{1,0:T(2,128)S(1)} %slice_reduce_fusion.2), channel_id=1, source_target_pairs={{0,32},{32,0},{64,96},{96,64},{128,160},{160,128},{192,224},{224,1... | collective-permute-start | bytes 3080 | tf_op jit(solution)/shard_map/ppermute | solution.py:42
  248.3 7.0 %collective-permute-start.24 = (f32[2,128]{1,0:T(2,128)S(1)}, f32[2,128]{1,0:T(2,128)S(1)}, u32[]{:S(2)}, u32[]{:S(2)}) collective-permute-start(f32[2,128]{1,0:T(2,128)S(1)} %add.184), channel_id=1, source_target_pairs={{0,64},{32,96},{64,0},{96,32},{128,192},{160,224},{192,128},{224,1... | collective-permute-start | bytes 3080 | tf_op jit(solution)/shard_map/ppermute | solution.py:42
  260.7 11.4 %collective-permute-start.26 = (f32[2,128]{1,0:T(2,128)S(1)}, f32[2,128]{1,0:T(2,128)S(1)}, u32[]{:S(2)}, u32[]{:S(2)}) collective-permute-start(f32[2,128]{1,0:T(2,128)S(1)} %add.186), channel_id=1, source_target_pairs={{0,256},{32,288},{64,320},{96,352},{128,384},{160,416},{192,448},{... | collective-permute-start | bytes 3080 | tf_op jit(solution)/shard_map/ppermute | solution.py:42
  266.3 6.1 %collective-permute-start.27 = (f32[2,2048]{1,0:T(2,128)S(1)}, f32[2,2048]{1,0:T(2,128)S(1)}, u32[]{:S(2)}, u32[]{:S(2)}) collective-permute-start(f32[2,2048]{1,0:T(2,128)S(1)} %slice.186), channel_id=1, source_target_pairs={{32,0},{64,32},{96,64},{128,96},{160,128},{192,160},{224,192},{256... | collective-permute-start | bytes 49160 | tf_op jit(solution)/shard_map/ppermute | solution.py:213
  268.3 7.7 %collective-permute-start.28 = (f32[2,2048]{1,0:T(2,128)S(1)}, f32[2,2048]{1,0:T(2,128)S(1)}, u32[]{:S(2)}, u32[]{:S(2)}) collective-permute-start(f32[2,2048]{1,0:T(2,128)S(1)} %slice.187), channel_id=1, source_target_pairs={{0,32},{32,64},{64,96},{96,128},{128,160},{160,192},{192,224},{224... | collective-permute-start | bytes 49160 | tf_op jit(solution)/shard_map/ppermute | solution.py:212
  298.9 6.2 %collective-permute-start.30 = (f32[2,128]{0,1:T(8,128)S(1)}, f32[2,128]{0,1:T(8,128)S(1)}, u32[]{:S(2)}, u32[]{:S(2)}) collective-permute-start(f32[2,128]{0,1:T(8,128)S(1)} %fusion.18), channel_id=1, source_target_pairs={{0,2},{1,3},{2,0},{3,1},{4,6},{5,7},{6,4},{7,5},{8,10},{9,11},{10,... | collective-permute-start | bytes 3080 | tf_op jit(solution)/shard_map/ppermute | solution.py:42
  305.1 7.4 %collective-permute-start.31 = (f32[2,128]{0,1:T(8,128)S(1)}, f32[2,128]{0,1:T(8,128)S(1)}, u32[]{:S(2)}, u32[]{:S(2)}) collective-permute-start(f32[2,128]{0,1:T(8,128)S(1)} %fusion.30), channel_id=1, source_target_pairs={{0,4},{1,5},{2,6},{3,7},{4,0},{5,1},{6,2},{7,3},{8,12},{9,13},{10,... | collective-permute-start | bytes 3080 | tf_op jit(solution)/shard_map/ppermute | solution.py:42
  312.5 11.9 %collective-permute-start.32 = (f32[2,128]{0,1:T(8,128)S(1)}, f32[2,128]{0,1:T(8,128)S(1)}, u32[]{:S(2)}, u32[]{:S(2)}) collective-permute-start(f32[2,128]{0,1:T(8,128)S(1)} %add.197), channel_id=1, source_target_pairs={{0,8},{1,9},{2,10},{3,11},{4,12},{5,13},{6,14},{7,15},{8,0},{9,1},... | collective-permute-start | bytes 3080 | tf_op jit(solution)/shard_map/ppermute | solution.py:42
  324.4 16.2 %collective-permute-start.33 = (f32[2,128]{0,1:T(8,128)S(1)}, f32[2,128]{0,1:T(8,128)S(1)}, u32[]{:S(2)}, u32[]{:S(2)}) collective-permute-start(f32[2,128]{0,1:T(8,128)S(1)} %add.198), channel_id=1, source_target_pairs={{0,16},{1,17},{2,18},{3,19},{4,20},{5,21},{6,22},{7,23},{8,24},{9,... | collective-permute-start | bytes 3080 | tf_op jit(solution)/shard_map/ppermute | solution.py:42
  340.6 6.6 %collective-permute-start.34 = (f32[2,128]{0,1:T(8,128)S(1)}, f32[2,128]{0,1:T(8,128)S(1)}, u32[]{:S(2)}, u32[]{:S(2)}) collective-permute-start(f32[2,128]{0,1:T(8,128)S(1)} %add.199), channel_id=1, source_target_pairs={{0,32},{32,0},{64,96},{96,64},{128,160},{160,128},{192,224},{224,1... | collective-permute-start | bytes 3080 | tf_op jit(solution)/shard_map/ppermute | solution.py:42
  347.3 7.7 %collective-permute-start.35 = (f32[2,128]{0,1:T(8,128)S(1)}, f32[2,128]{0,1:T(8,128)S(1)}, u32[]{:S(2)}, u32[]{:S(2)}) collective-permute-start(f32[2,128]{0,1:T(8,128)S(1)} %add.200), channel_id=1, source_target_pairs={{0,64},{32,96},{64,0},{96,32},{128,192},{160,224},{192,128},{224,1... | collective-permute-start | bytes 3080 | tf_op jit(solution)/shard_map/ppermute | solution.py:42
  355.0 6.2 %collective-permute-start.36 = (f32[2,128]{0,1:T(8,128)S(1)}, f32[2,128]{0,1:T(8,128)S(1)}, u32[]{:S(2)}, u32[]{:S(2)}) collective-permute-start(f32[2,128]{0,1:T(8,128)S(1)} %add.201), channel_id=1, source_target_pairs={{0,128},{32,160},{64,192},{96,224},{128,0},{160,32},{192,64},{224,... | collective-permute-start | bytes 3080 | tf_op jit(solution)/shard_map/ppermute | solution.py:42
  361.1 7.7 %collective-permute-start.37 = (f32[2,128]{0,1:T(8,128)S(1)}, f32[2,128]{0,1:T(8,128)S(1)}, u32[]{:S(2)}, u32[]{:S(2)}) collective-permute-start(f32[2,128]{0,1:T(8,128)S(1)} %add.202), channel_id=1, source_target_pairs={{0,256},{32,288},{64,320},{96,352},{128,384},{160,416},{192,448},{... | collective-permute-start | bytes 3080 | tf_op jit(solution)/shard_map/ppermute | solution.py:42
  (7 other events, 129.7 us)

commit v2 on v0

--- a/solution.py
+++ b/solution.py
@@ -1,9 +1,23 @@
+import functools
+
 import jax
 import jax.numpy as jnp
 from jax import lax
+from jax.experimental import pallas as pl
+from jax.experimental.pallas import tpu as pltpu
 from jax.sharding import PartitionSpec as P
 
 ITERS = 3
+LANES = 128
+SCALE = 4.0**0.2
+HEAD = 5.0 / SCALE**4
+FAR = 1e18
+PAIRS = [(i, j) for i in range(ITERS + 1) for j in range(i, ITERS + 1)]
+SUM_ROWS = 24
+OK_ROW = 2 * len(PAIRS)
+GUARD = 3e-5
+SMEM = pltpu.MemorySpace.SMEM
+VMEM = pltpu.MemorySpace.VMEM
 
 
 def padded(array, sides, width):
@@ -32,7 +46,7 @@
     return lax.optimization_barrier(values.astype(jnp.bfloat16)).astype(jnp.float32)
 
 
-def body(right_side, noise_var, coords, counts, pair_list):
+def any_graph(right_side, noise_var, coords, counts, pair_list):
     tile_count = lax.axis_size("tile")
     tile_len = right_side.shape[1]
     columns = right_side.shape[0]
@@ -47,11 +61,8 @@
         city_shift = (pair_kind == 2).astype(jnp.int32) - (pair_kind == 3).astype(jnp.int32)
         return second_tile + tile_count * (1 + city_shift)
 
-    residual = right_side * valid_mask[None, :]
-    direction = residual
-    solution_field = jnp.zeros_like(residual)
-    norm_now = lax.psum(jnp.sum(residual * residual, axis=1), ("city", "tile"))
-    for iteration in range(ITERS):
+    def iterate(carry, _):
+        residual, direction, solution_field, norm_now = carry
         own_dirs = direction.astype(jnp.bfloat16)
         city_dirs = lax.all_gather(own_dirs[None], "tile", axis=0, tiled=True)
         wide_dirs = padded(city_dirs, (("city", 0),), tile_count)
@@ -113,12 +124,465 @@
         step_size = norm_now / curvature
         solution_field = solution_field + step_size[:, None] * direction
         residual = residual - step_size[:, None] * applied
-        if iteration + 1 < ITERS:
-            norm_next = lax.psum(jnp.sum(residual * residual, axis=1), ("city", "tile"))
-        if iteration + 1 < ITERS:
-            direction = residual + (norm_next / norm_now)[:, None] * direction
-            norm_now = norm_next
+        norm_next = lax.psum(jnp.sum(residual * residual, axis=1), ("city", "tile"))
+        direction = residual + (norm_next / norm_now)[:, None] * direction
+        return (residual, direction, solution_field, norm_next), None
+
+    residual = right_side * valid_mask[None, :]
+    norm_now = lax.psum(jnp.sum(residual * residual, axis=1), ("city", "tile"))
+    carry = (residual, residual, jnp.zeros_like(residual), norm_now)
+    (residual, _, solution_field, _), _ = lax.scan(iterate, carry, None, length=ITERS)
     return (solution_field, residual)
+
+
+def folded(ref, row):
+    length = ref.shape[1]
+    return jnp.concatenate(
+        [ref[row : row + 1, left : left + LANES] for left in range(0, length, LANES)], axis=0
+    )
+
+
+def columns_of(rows):
+    missing = LANES - rows.shape[0]
+    return jnp.transpose(jnp.concatenate([rows, jnp.zeros((missing, LANES), rows.dtype)], axis=0))
+
+
+def spread(rows, ref):
+    turned = columns_of(rows)
+    for c in range(rows.shape[0]):
+        ref[c * LANES : (c + 1) * LANES, :] = jnp.broadcast_to(
+            turned[:, c : c + 1], (LANES, LANES)
+        )
+
+
+def taken(values, source):
+    chunk, lane = source // LANES, source % LANES
+    result = jnp.zeros_like(values)
+    for c in range(values.shape[0]):
+        row = jnp.broadcast_to(values[c : c + 1, :], values.shape)
+        result = jnp.where(chunk == c, jnp.take_along_axis(row, lane, axis=1), result)
+    return result
+
+
+def arrange_kernel(place, right_ref, noise_ref, coords_ref, table_ref, out_ref, rank_ref, wide):
+    length = right_ref.shape[1]
+    chunks = length // LANES
+    lane = lax.broadcasted_iota(jnp.int32, (chunks, LANES), 1)
+    index = lax.broadcasted_iota(jnp.int32, (chunks, LANES), 0) * LANES + lane
+    valid = index < place[1]
+    x, y = folded(coords_ref, 0), folded(coords_ref, 1)
+    noise = jnp.where(valid, folded(noise_ref, 0), -1.0)
+    right = [jnp.where(valid, folded(right_ref, r), 0.0) for r in range(2)]
+
+    least = jnp.min(jnp.where(valid, y, FAR), keepdims=True)
+    most = jnp.max(jnp.where(valid, y, -FAR), keepdims=True)
+    bins = float(length - 1)
+    level = jnp.floor((y - least) * (bins / jnp.maximum(most - least, 1e-6)))
+    level = jnp.where(valid, jnp.clip(level, 0.0, bins), bins + 1.0)
+    key = level * float(length) + index.astype(jnp.float32)
+
+    def counted(rows, hit):
+        def step(c, sums):
+            column = wide[pl.ds(pl.multiple_of(c * LANES, LANES), LANES), :]
+            found = []
+            for r in range(chunks):
+                terms = hit(column, rows[r : r + 1, :], c)
+                found.append(sums[r] + jnp.sum(terms.reshape(LANES // 8, 8, LANES), axis=0))
+            return tuple(found)
+
+        zero = jnp.zeros((8, LANES), jnp.float32)
+        sums = lax.fori_loop(0, chunks, step, (zero,) * chunks)
+        return jnp.concatenate([jnp.sum(s, axis=0, keepdims=True) for s in sums], axis=0)
+
+    spread(key, wide)
+    rank = counted(key, lambda column, row, c: jnp.where(column < row, 1.0, 0.0))
+    spread(rank, wide)
+    within = lax.broadcasted_iota(jnp.int32, (LANES, LANES), 0)
+    source = counted(
+        index.astype(jnp.float32),
+        lambda column, row, c: jnp.where(
+            column == row, (within + c * LANES).astype(jnp.float32), 0.0
+        ),
+    ).astype(jnp.int32)
+    rank_ref[...] = rank.astype(jnp.int32)
+    for place_of, rows in enumerate((x, y, right[0], right[1], noise)):
+        out_ref[place_of * chunks : (place_of + 1) * chunks, :] = taken(rows, source)
+    out_ref[5 * chunks : 5 * chunks + 8, :] = table_ref[...]
+
+
+def order_kernel(own, table, gathered, mine_ref, info, near_a, near_b, degree, order, sem):
+    tiles = table.shape[0]
+
+    def clear(t, _):
+        degree[t] = 0
+        near_a[t] = -1
+        near_b[t] = -1
+        return 0
+
+    lax.fori_loop(0, tiles, clear, 0)
+
+    def join(a, b):
+        count = degree[a]
+
+        @pl.when(count == 0)
+        def _():
+            near_a[a] = b
+
+        @pl.when(count == 1)
+        def _():
+            near_b[a] = b
+
+        degree[a] = count + 1
+
+    for slot in range(8):
+        info[slot] = 0
+    info[5] = -1
+    info[6] = -1
+
+    def read(t, _):
+        for slot in range(table.shape[1] // 3):
+            kind = table[t, 3 * slot + 2]
+
+            @pl.when(kind > 0)
+            def _():
+                a, b = table[t, 3 * slot], table[t, 3 * slot + 1]
+
+                @pl.when(kind == 2)
+                def _():
+                    info[5] = a
+
+                @pl.when(kind == 3)
+                def _():
+                    info[6] = a
+
+                @pl.when((kind == 1) & (a == b))
+                def _():
+                    info[3] = info[3] + 1
+
+                @pl.when((kind == 1) & (a != b))
+                def _():
+                    info[4] = info[4] + 1
+                    join(a, b)
+                    join(b, a)
+
+        return 0
+
+    lax.fori_loop(0, tiles, read, 0)
+    selfs, edges, to_next, to_prev = info[3], info[4], info[5], info[6]
+
+    def end_of(t, best):
+        fits = (degree[t] <= 1) & (t != to_next) & (best < 0)
+        return jnp.where(fits, t, best)
+
+    start = lax.fori_loop(0, tiles, end_of, to_prev)
+    complete = (start >= 0) & (selfs == tiles) & (edges == tiles - 1)
+
+    def walk(p, carry):
+        before, tile, good = carry
+        order[p] = tile
+        good = good & (degree[tile] <= 2)
+
+        @pl.when(tile == own[0])
+        def _():
+            info[1] = p
+
+        a, b = near_a[tile], near_b[tile]
+        following = jnp.where(a != before, a, b)
+        good = good & ((following >= 0) | (p == tiles - 1))
+        return tile, jnp.maximum(following, 0), good
+
+    first = jnp.maximum(start, 0)
+    _, _, good = lax.fori_loop(0, tiles, walk, (jnp.int32(-1), first, complete))
+    last = order[tiles - 1]
+    good = good & ((to_prev < 0) | (degree[first] <= 1)) & (degree[last] <= 1)
+    good = good & ((to_next < 0) | (last == to_next))
+    tile = order[own[0]]
+    info[0] = tile
+    info[2] = good.astype(jnp.int32)
+    info[3] = ((own[0] > 0) | (to_prev >= 0)).astype(jnp.int32)
+    info[4] = ((own[0] < tiles - 1) | (to_next >= 0)).astype(jnp.int32)
+    copy = pltpu.make_async_copy(gathered.at[tile], mine_ref, sem)
+    copy.start()
+    copy.wait()
+
+
+def apply_kernel(
+    base, info, mine, before, after, vec_0, vec_1, vec_2, out_ref, near_x, near_y, far, low, high
+):
+    chunks = out_ref.shape[0] // 2
+    tiles, vecs = (mine, before, after), (vec_0, vec_1, vec_2)
+    origin_x, origin_y = mine[0:1, 0:1], mine[chunks : chunks + 1, 0:1]
+
+    def box(ref):
+        good = ref[4 * chunks : 5 * chunks, :] >= 0.0
+        sides = []
+        for row in (0, chunks):
+            values = ref[row : row + chunks, :]
+            sides.append(jnp.min(jnp.where(good, values, FAR), axis=1, keepdims=True))
+            sides.append(jnp.max(jnp.where(good, values, -FAR), axis=1, keepdims=True))
+        return sides
+
+    near_box = box(mine)
+    for slot, ref in enumerate(tiles):
+        far_box = near_box if slot == 0 else box(ref)
+        least = jnp.full((chunks, 1), float(chunks), jnp.float32)
+        most = jnp.zeros((chunks, 1), jnp.float32)
+        for c in range(chunks):
+            f = [side[c : c + 1, :] for side in far_box]
+            gap_x = jnp.maximum(jnp.maximum(near_box[0] - f[1], f[0] - near_box[1]), 0.0)
+            gap_y = jnp.maximum(jnp.maximum(near_box[2] - f[3], f[2] - near_box[3]), 0.0)
+            close = gap_x * gap_x + gap_y * gap_y < 1.0001
+            least = jnp.where(close, jnp.minimum(least, float(c // 2)), least)
+            most = jnp.where(close, float(c // 2 + 1), most)
+        for c in range(chunks):
+            low[slot, c] = jnp.max(least[c : c + 1, :]).astype(jnp.int32)
+            top = jnp.max(most[c : c + 1, :]).astype(jnp.int32)
+            high[slot, c] = top if slot == 0 else top * info[2 + slot]
+        far[slot, 0:chunks, :] = (ref[0:chunks, :] - origin_x) * SCALE
+        far[slot, chunks : 2 * chunks, :] = (ref[chunks : 2 * chunks, :] - origin_y) * SCALE
+    spread(far[0, 0:chunks, :], near_x)
+    spread(far[0, chunks : 2 * chunks, :], near_y)
+    groups = LANES // 8
+
+    def near_chunk(i, _):
+        sums = tuple(jnp.zeros((8, LANES), jnp.float32) for _ in range(2 * groups))
+        for slot in range(3):
+
+            def far_chunks(j, sums):
+                found = list(sums)
+                cells = []
+                for h in range(2):
+                    c = 2 * j + h
+                    cells.append(
+                        (
+                            far[slot, pl.ds(c, 1), :],
+                            far[slot, pl.ds(chunks + c, 1), :],
+                            vecs[slot][pl.ds(base + c, 1), :],
+                            vecs[slot][pl.ds(base + chunks + c, 1), :],
+                        )
+                    )
+                for g in range(groups):
+                    here = pl.ds(pl.multiple_of(i * LANES + 8 * g, 8), 8)
+                    x, y = near_x[here, :], near_y[here, :]
+                    for far_x, far_y, v_0, v_1 in cells:
+                        across, along = x - far_x, y - far_y
+                        square = jnp.maximum(across * across + along * along, 1e-30)
+                        inside = jnp.maximum(SCALE - square * lax.rsqrt(square), 0.0)
+                        power = inside * inside
+                        value = power * power * (HEAD - inside)
+                        found[2 * g] = found[2 * g] + value * v_0
+                        found[2 * g + 1] = found[2 * g + 1] + value * v_1
+                return tuple(found)
+
+            sums = lax.fori_loop(low[slot, i], high[slot, i], far_chunks, sums)
+        noise = mine[pl.ds(4 * chunks + i, 1), :]
+        for r in range(2):
+            block = jnp.concatenate(sums[r::2], axis=0)
+            total = jnp.sum(jnp.transpose(block), axis=0, keepdims=True)
+            own = vec_0[pl.ds(base + r * chunks + i, 1), :]
+            out_ref[pl.ds(r * chunks + i, 1), :] = jnp.where(noise >= 0.0, total + noise * own, own)
+        return 0
+
+    lax.fori_loop(0, chunks, near_chunk, 0)
+
+
+def sums_kernel(info, mine, vec_1, vec_2, vec_3, out_ref):
+    chunks = vec_1.shape[0] // 2
+    vecs = (mine[2 * chunks : 4 * chunks, :], vec_1[...], vec_2[...], vec_3[...])
+    rows = []
+    for r in range(2):
+        half = [v[r * chunks : (r + 1) * chunks, :] for v in vecs]
+        rows += [jnp.sum(half[i] * half[j], axis=0, keepdims=True) for i, j in PAIRS]
+    rows.append(jnp.full((1, LANES), 1.0, jnp.float32) * info[2].astype(jnp.float32))
+    rows.append(jnp.zeros((SUM_ROWS - len(rows), LANES), jnp.float32))
+    out_ref[...] = jnp.concatenate(rows, axis=0)
+
+
+def finish_kernel(devices, info, vecs_ref, sums_ref, home, rank, field_ref, residual_ref, ok_ref):
+    chunks = rank.shape[0]
+    total = jnp.sum(jnp.sum(sums_ref[...], axis=0), axis=1, keepdims=True)
+    good = total[OK_ROW : OK_ROW + 1, :] == float(devices * LANES)
+    places = rank[...]
+    for r in range(2):
+        gram = {}
+        for k, (i, j) in enumerate(PAIRS):
+            row = r * len(PAIRS) + k
+            gram[i, j] = gram[j, i] = total[row : row + 1, :]
+
+        def form(a, b):
+            terms = [a[i] * b[j] * gram[i, j] for i in a for j in b]
+            value, size = terms[0], jnp.abs(terms[0])
+            for term in terms[1:]:
+                value, size = value + term, size + jnp.abs(term)
+            return value, value > GUARD * size
+
+        def plus(a, scale, b):
+            keys = sorted(set(a) | set(b))
+            return {
+                k: a[k] + scale * b[k] if k in a and k in b else (a[k] if k in a else scale * b[k])
+                for k in keys
+            }
+
+        one = jnp.ones((1, 1), jnp.float32)
+        res, direction, field = {0: one}, {0: one}, {}
+        norm, fine = form(res, res)
+        good = good & fine
+        for iteration in range(ITERS):
+            image = {k + 1: v for k, v in direction.items()}
+            curve, fine = form(direction, image)
+            good = good & fine
+            step = norm / curve
+            field = plus(field, step, direction)
+            res = plus(res, -step, image)
+            if iteration + 1 < ITERS:
+                new, fine = form(res, res)
+                good = good & fine
+                direction = plus(res, new / norm, direction)
+                norm = new
+
+        def vec(k):
+            if k == 0:
+                return home[(2 + r) * chunks : (3 + r) * chunks, :]
+            row = (2 * (k - 1) + r) * chunks
+            return vecs_ref[0, row : row + chunks, :]
+
+        for ref, weights in ((field_ref, field), (residual_ref, res)):
+            values = taken(sum(w * vec(k) for k, w in weights.items()), places)
+            for c in range(chunks):
+                ref[r : r + 1, c * LANES : (c + 1) * LANES] = values[c : c + 1, :]
+    ok_ref[...] = jnp.where(good, 1.0, 0.0) * jnp.ones((8, LANES), jnp.float32)
+
+
+def whole(shape):
+    return pl.BlockSpec(shape, lambda i, *_: (0,) * len(shape))
+
+
+def params(mib=16):
+    return pltpu.CompilerParams(vmem_limit_bytes=mib * 1024 * 1024)
+
+
+def body(right_side, noise_var, coords, counts, pair_list):
+    own = lax.axis_index("tile").astype(jnp.int32)
+    tiles, cities = lax.axis_size("tile"), lax.axis_size("city")
+    length = right_side.shape[1]
+    chunks = length // LANES
+    rows = 5 * chunks + 8
+    table = pair_list.reshape(1, -1).astype(jnp.float32)
+    entries = table.shape[1]
+    table = jnp.pad(table, ((0, 7), (0, LANES - entries)))
+    f32 = functools.partial(jax.ShapeDtypeStruct, dtype=jnp.float32)
+
+    home, rank = pl.pallas_call(
+        arrange_kernel,
+        grid_spec=pltpu.PrefetchScalarGridSpec(
+            num_scalar_prefetch=1,
+            grid=(1,),
+            in_specs=[
+                whole((2, length)),
+                whole((1, length)),
+                pl.BlockSpec((2, length), lambda i, place: (0, place[0])),
+                whole((8, LANES)),
+            ],
+            out_specs=[whole((rows, LANES)), whole((chunks, LANES))],
+            scratch_shapes=[pltpu.VMEM((length, LANES), jnp.float32)],
+        ),
+        out_shape=[f32((rows, LANES)), jax.ShapeDtypeStruct((chunks, LANES), jnp.int32)],
+        compiler_params=params(),
+        name="arrange",
+    )(jnp.stack([own, counts[0]]), right_side, noise_var[None, :], coords, table)
+
+    gathered = lax.all_gather(home, "tile")
+    city_table = gathered[:, 5 * chunks, :entries].astype(jnp.int32)
+    mine, info = pl.pallas_call(
+        order_kernel,
+        in_specs=[
+            pl.BlockSpec(memory_space=SMEM),
+            pl.BlockSpec(memory_space=SMEM),
+            pl.BlockSpec(memory_space=pl.ANY),
+        ],
+        out_specs=[pl.BlockSpec(memory_space=VMEM), pl.BlockSpec(memory_space=SMEM)],
+        out_shape=[f32((rows, LANES)), jax.ShapeDtypeStruct((8,), jnp.int32)],
+        scratch_shapes=[pltpu.SMEM((tiles,), jnp.int32)] * 4 + [pltpu.SemaphoreType.DMA],
+        compiler_params=params(),
+        name="order",
+    )(own[None], city_table, gathered)
+
+    forward = [(i, i + 1) for i in range(tiles * cities - 1)]
+    backward = [(j, i) for i, j in forward]
+
+    def neighbours(block):
+        axes = ("city", "tile")
+        return lax.ppermute(block, axes, forward), lax.ppermute(block, axes, backward)
+
+    def apply(ends, vecs, base):
+        size = vecs[0].shape[0]
+        return pl.pallas_call(
+            functools.partial(apply_kernel, base),
+            grid_spec=pltpu.PrefetchScalarGridSpec(
+                num_scalar_prefetch=1,
+                grid=(1,),
+                in_specs=[whole((rows, LANES))] * 3 + [whole((size, LANES))] * 3,
+                out_specs=whole((2 * chunks, LANES)),
+                scratch_shapes=[
+                    pltpu.VMEM((length, LANES), jnp.float32),
+                    pltpu.VMEM((length, LANES), jnp.float32),
+                    pltpu.VMEM((3, 2 * chunks, LANES), jnp.float32),
+                    pltpu.SMEM((3, chunks), jnp.int32),
+                    pltpu.SMEM((3, chunks), jnp.int32),
+                ],
+            ),
+            out_shape=f32((2 * chunks, LANES)),
+            compiler_params=params(),
+            name="apply",
+        )(info, mine, *ends, *vecs)
+
+    ends = neighbours(mine)
+    vec_1 = apply(ends, (mine, *ends), 2 * chunks)
+    vec_2 = apply(ends, (vec_1, *neighbours(vec_1)), 0)
+    vec_3 = apply(ends, (vec_2, *neighbours(vec_2)), 0)
+
+    sums = pl.pallas_call(
+        sums_kernel,
+        grid_spec=pltpu.PrefetchScalarGridSpec(
+            num_scalar_prefetch=1,
+            grid=(1,),
+            in_specs=[whole((rows, LANES))] + [whole((2 * chunks, LANES))] * 3,
+            out_specs=whole((SUM_ROWS, LANES)),
+        ),
+        out_shape=f32((SUM_ROWS, LANES)),
+        compiler_params=params(),
+        name="sums",
+    )(info, mine, vec_1, vec_2, vec_3)
+    sums = jnp.sum(lax.all_gather(sums, "city"), axis=0)
+    back = lax.all_gather(jnp.concatenate([vec_1, vec_2, vec_3, sums], axis=0), "tile")
+    size = 6 * chunks
+    field, residual, good = pl.pallas_call(
+        functools.partial(finish_kernel, tiles * cities),
+        grid_spec=pltpu.PrefetchScalarGridSpec(
+            num_scalar_prefetch=1,
+            grid=(1,),
+            in_specs=[
+                pl.BlockSpec((1, size, LANES), lambda i, info: (info[1], 0, 0)),
+                pl.BlockSpec((tiles, SUM_ROWS, LANES), lambda i, info: (0, size // SUM_ROWS, 0)),
+                whole((rows, LANES)),
+                whole((chunks, LANES)),
+            ],
+            out_specs=[whole((2, length)), whole((2, length)), whole((8, LANES))],
+        ),
+        out_shape=[f32((2, length)), f32((2, length)), f32((8, LANES))],
+        compiler_params=params(),
+        name="finish",
+    )(info, back, back, home, rank)
+    return lax.cond(
+        good[0, 0] > 0.0,
+        lambda *args: (field, residual),
+        any_graph,
+        right_side,
+        noise_var,
+        coords,
+        counts,
+        pair_list,
+    )
 
 
 def solution(mesh):

time: 1250 us -> 278 us (0.22); the launches traced: 1240 us -> 277 us
  blocking collectives: 837 us -> 19.8 us
  matrix products: 136 us -> 0 us
  waiting for transfers between devices: 53 us -> 161 us
  starting transfers between devices: 111 us -> 13.8 us
  loops' own time: 70.6 us -> 0.19 us
  Pallas kernels: 0 us -> 61.5 us
  local copies, waits for them, and re-layouts: 18.8 us -> 3.64 us
  between operations: 1.95 us -> 15.5 us
    psum x5 -> x0, blocking collectives: 514 us -> none  [the longest x2 209 us: body(): curvature = lax.psum(jnp.sum(direction * applied, axis=1), ('city', 'tile'))]
    all_to_all x2 -> x0, blocking collectives: 227 us -> none  [body(): lax.all_to_all(buffer.astype(jnp.bfloat16), 'tile', split_axis=0, concat_...]
    all_gather x0 -> x2, waiting for transfers between devices: none -> 152 us  [the longest x1 77 us: body(): gathered = lax.all_gather(home, 'tile')]
    dot_general x48 -> x0, matrix products: 136 us -> none  [the longest x24 67.9 us: compute(): lax.dot_general(far_vec, kernel, (((1,), (1,)), ((), ())), preferred_elem...]
    all_to_all x1 -> x0, starting transfers between devices: 92.8 us -> none  [body(): lax.all_to_all(buffer.astype(jnp.bfloat16), 'tile', split_axis=0, concat_...]
    all_gather x3 -> x1, blocking collectives: 96 us -> 19.8 us  [body(): sums = jnp.sum(lax.all_gather(sums, 'city'), axis=0)]
    another operation x18 -> x1, loops' own time: 70.6 us -> 0.19 us  [body(): lax.cond(good[0, 0] > 0.0, lambda *args: (field, residual), any_graph, ri...]
    pallas_call x0 -> x7, Pallas kernels: none -> 61.5 us  [the longest x3 45.3 us: apply(): pl.pallas_call(functools.partial(apply_kernel, base), grid_spec=pltpu.Pre...]
  transfers between devices with their start and end apart: 9 -> 8, of which waited for: 8 -> 5; matrix products, arithmetic and copies ran while one was open for 0% -> 0% of each run, Pallas kernels for 0% -> 0%
where the time goes in v2:
time: 278 us; the launch traced here: 277 us
  waiting for transfers between devices  161 us (58%)
  Pallas kernels  61.5 us (22%)
  blocking collectives  19.8 us (7%)
  between operations  15.5 us (6%)
  starting transfers between devices  13.8 us (5%)
  local copies, waits for them, and re-layouts  3.64 us (1%)
    all_gather x1, waiting for transfers between devices, body(): gathered = lax.all_gather(home, 'tile')  77 us
    all_gather x1, waiting for transfers between devices, body(): lax.all_gather(jnp.concatenate([vec_1, vec_2, vec_3, sums], axis=0), 'tile')  74.8 us
    pallas_call x3, Pallas kernels, apply(): pl.pallas_call(functools.partial(apply_kernel, base), grid_spec=pltpu.Pre...  45.3 us
    all_gather x1, blocking collectives, body(): sums = jnp.sum(lax.all_gather(sums, 'city'), axis=0)  19.8 us
    ppermute x3, waiting for transfers between devices, neighbours(): lax.ppermute(block, axes, backward)  8.7 us
    pallas_call x1, Pallas kernels, body(): pl.pallas_call(arrange_kernel, grid_spec=pltpu.PrefetchScalarGridSpec(num...  7.05 us
    ppermute x3, starting transfers between devices, neighbours(): lax.ppermute(block, axes, forward)  7.04 us
    ppermute x3, starting transfers between devices, neighbours(): lax.ppermute(block, axes, backward)  6.73 us
  transfers between devices with their start and end apart: 8, of which 5 were waited for; matrix products, arithmetic and copies ran while one was open for 0% of the time, Pallas kernels for 0%

profile of v2, /device:TPU:1, one launch (start us, length us, event | category | flops | bytes accessed | tf_op | source)
XLA Modules:
  0.0 277.4 jit_solution(7715171133444109046)
XLA Ops:
  7.2 0.0 all-gather.11.cloned.1.call-start
  7.9 0.7 convert_element_type.107
  8.5 0.1 copy.14
  8.6 0.1 convert_element_type.108
  8.7 0.1 pad_add_fusion.place
  8.8 7.0 %arrange.1 = (f32[88,128]{1,0:T(8,128)}, s32[16,128]{1,0:T(8,128)S(1)}) custom-call(s32[2]{0:T(128)S(1)} %pad_add_fusion.place, f32[2,2048]{1,0:T(2,128)} %right_ref.1, f32[1,2048]{1,0:T(1,128)} %bitcast.91, f32[2,65536]{1,0:T(2,128)} %coords_ref.1, f32[8,128]{1,0:T(8,128)S(1)} %pad.4.table_ref), custom_call_target="tpu_custom_call" | custom-call | tf_op jit(solution)/shard_map/arrange/pallas_call | solution.py:475
  15.9 0.0 all-gather.11.cloned.1.call-update
  15.9 0.0 all-gather.13.cloned.1.call-start
  15.9 77.0 %all-gather.11.cloned.1.call-done = f32[2816,128]{1,0:T(8,128)} async-done(((f32[88,128]{1,0:T(8,128)}), f32[2816,128]{1,0:T(8,128)}) %all-gather.11.cloned.1.call-update) | async-done | bytes 1441808 | tf_op jit(solution)/shard_map/all_gather | solution.py:494
  93.0 0.9 slice_convert_fusion
  93.9 1.4 copy-done.1
  95.3 6.1 %order.1 = (f32[88,128]{1,0:T(8,128)S(1)}, s32[8]{0:T(128)S(1)}) custom-call(s32[1]{0:T(128)} %bitcast.21.own, s32[32,15]{1,0:T(8,128)S(1)} %bitcast.57, f32[32,88,128]{2,1,0:T(8,128)S(1)} %bitcast.56), custom_call_target="tpu_custom_call" | custom-call | tf_op jit(solution)/shard_map/order/pallas_call | solution.py:496
  101.3 3.2 %collective-permute-start.4 = (f32[88,128]{1,0:T(8,128)S(1)}, f32[88,128]{1,0:T(8,128)S(1)}, u32[]{:S(2)}, u32[]{:S(2)}) collective-permute-start(f32[88,128]{1,0:T(8,128)S(1)} %get-tuple-element.273.mine.vec_0), channel_id=1, source_target_pairs={{0,1},{1,2},{2,3},{3,4},{4,5},{5,6},{6,7},{7,8},{8,9},{9,10},{10,1... | collective-permute-start | bytes 135176 | tf_op jit(solution)/shard_map/ppermute | solution.py:515
  104.5 1.9 collective-permute-start.5
  106.5 3.4 %collective-permute-done.5.after.vec_2 = f32[88,128]{1,0:T(8,128)S(1)} collective-permute-done((f32[88,128]{1,0:T(8,128)S(1)}, f32[88,128]{1,0:T(8,128)S(1)}, u32[]{:S(2)}, u32[]{:S(2)}) %collective-permute-start.5) | collective-permute-done | bytes 45088 | tf_op jit(solution)/shard_map/ppermute | solution.py:515
  109.9 15.1 %apply.3.vec_0.vec_1 = f32[32,128]{1,0:T(8,128)S(1)} custom-call(s32[8]{0:T(128)S(1)} %get-tuple-element.272.info, f32[88,128]{1,0:T(8,128)S(1)} %get-tuple-element.273.mine.vec_0, f32[88,128]{1,0:T(8,128)S(1)} %collective-permute-done.4.before.vec_1, f32[88,128]{1,0:T(8,128)S(1)} %collective-permute-done.5.after.vec_2, ...), custom_call_target="tpu_custom_call" | custom-call | tf_op jit(solution)/shard_map/apply/pallas_call | solution.py:519
  125.0 1.9 collective-permute-start.6
  127.0 2.4 collective-permute-start.7
  129.4 2.6 collective-permute-done.7.vec_2
  132.0 15.1 %apply.4.vec_0.vec_2 = f32[32,128]{1,0:T(8,128)S(1)} custom-call(s32[8]{0:T(128)S(1)} %get-tuple-element.272.info, f32[88,128]{1,0:T(8,128)S(1)} %get-tuple-element.273.mine.vec_0, f32[88,128]{1,0:T(8,128)S(1)} %collective-permute-done.4.before.vec_1, f32[88,128]{1,0:T(8,128)S(1)} %collective-permute-done.5.after.vec_2, f32[32,128]{1,0:T(8,128)S(1)} %apply.3.vec_0.vec_1, ...), custom_call_target="tpu_custom_call" | custom-call | tf_op jit(solution)/shard_map/apply/pallas_call | solution.py:519
  147.1 1.9 collective-permute-start.8
  149.1 2.4 collective-permute-start.9
  151.5 2.6 collective-permute-done.9.vec_2
  154.1 15.1 %apply.5.vec_3 = f32[32,128]{1,0:T(8,128)S(1)} custom-call(s32[8]{0:T(128)S(1)} %get-tuple-element.272.info, f32[88,128]{1,0:T(8,128)S(1)} %get-tuple-element.273.mine.vec_0, f32[88,128]{1,0:T(8,128)S(1)} %collective-permute-done.4.before.vec_1, f32[88,128]{1,0:T(8,128)S(1)} %collective-permute-done.5.after.vec_2, f32[32,128]{1,0:T(8,128)S(1)} %apply.4.vec_0.vec_2, ...), custom_call_target="tpu_custom_call" | custom-call | tf_op jit(solution)/shard_map/apply/pallas_call | solution.py:519
  169.2 0.6 sums.1
  169.8 19.8 %all-gather.2 = f32[384,128]{1,0:T(8,128)S(1)} all-gather(f32[24,128]{1,0:T(8,128)S(1)} %sums.1), channel_id=4, replica_groups=mesh['city'=16,'tile'=32] {'city'}, dimensions={0}, use_global_device_ids=true | all-gather | bytes 208896 | tf_op jit(solution)/shard_map/all_gather | solution.py:556
  189.6 0.6 pad_maximum_fusion.3
  190.2 74.8 %all-gather.13.cloned.1.call-done = f32[3840,128]{1,0:T(8,128)} async-done(((f32[120,128]{1,0:T(8,128)}), f32[3840,128]{1,0:T(8,128)}) %all-gather.13.cloned.1.call-update) | async-done | bytes 1966096 | tf_op jit(solution)/shard_map/all_gather | solution.py:557
  265.0 1.5 copy-done
  266.6 2.5 finish.1
  269.1 0.5 slice.124
  270.3 0.2 conditional.2
  (16 shorter events, 0.1 us)
Async XLA Ops:
  7.2 85.8 %all-gather.11.cloned.1.call-start = ((), (), s32[]{:S(2)}) async-start(), calls=%async_computation.1 | async-start | bytes 1486848 | tf_op jit(solution)/shard_map/all_gather | solution.py:494
  15.9 249.2 %all-gather.13.cloned.1.call-start = ((), (), s32[]{:S(2)}) async-start(), calls=%async_computation.2 | async-start | bytes 2027520 | tf_op jit(solution)/shard_map/all_gather | solution.py:557
  93.9 1.4 copy-start.1
  101.3 5.1 %collective-permute-start.4 = (f32[88,128]{1,0:T(8,128)S(1)}, f32[88,128]{1,0:T(8,128)S(1)}, u32[]{:S(2)}, u32[]{:S(2)}) collective-permute-start(f32[88,128]{1,0:T(8,128)S(1)} %get-tuple-element.273.mine.vec_0), channel_id=1, source_target_pairs={{0,1},{1,2},{2,3},{3,4},{4,5},{5,6},{6,7},{7,8},{8,9},{9,10},{10,1... | collective-permute-start | bytes 135176 | tf_op jit(solution)/shard_map/ppermute | solution.py:515
  104.5 5.4 %collective-permute-start.5 = (f32[88,128]{1,0:T(8,128)S(1)}, f32[88,128]{1,0:T(8,128)S(1)}, u32[]{:S(2)}, u32[]{:S(2)}) collective-permute-start(f32[88,128]{1,0:T(8,128)S(1)} %get-tuple-element.273.mine.vec_0), channel_id=1, source_target_pairs={{1,0},{2,1},{3,2},{4,3},{5,4},{6,5},{7,6},{8,7},{9,8},{10,9},{11,1... | collective-permute-start | bytes 135176 | tf_op jit(solution)/shard_map/ppermute | solution.py:515
  125.0 4.3 %collective-permute-start.6 = (f32[32,128]{1,0:T(8,128)S(1)}, f32[32,128]{1,0:T(8,128)S(1)}, u32[]{:S(2)}, u32[]{:S(2)}) collective-permute-start(f32[32,128]{1,0:T(8,128)S(1)} %apply.3.vec_0.vec_1), channel_id=1, source_target_pairs={{0,1},{1,2},{2,3},{3,4},{4,5},{5,6},{6,7},{7,8},{8,9},{9,10},{10,1... | collective-permute-start | bytes 49160 | tf_op jit(solution)/shard_map/ppermute | solution.py:515
  127.0 5.1 %collective-permute-start.7 = (f32[32,128]{1,0:T(8,128)S(1)}, f32[32,128]{1,0:T(8,128)S(1)}, u32[]{:S(2)}, u32[]{:S(2)}) collective-permute-start(f32[32,128]{1,0:T(8,128)S(1)} %apply.3.vec_0.vec_1), channel_id=1, source_target_pairs={{1,0},{2,1},{3,2},{4,3},{5,4},{6,5},{7,6},{8,7},{9,8},{10,9},{11,1... | collective-permute-start | bytes 49160 | tf_op jit(solution)/shard_map/ppermute | solution.py:515
  147.1 4.3 %collective-permute-start.8 = (f32[32,128]{1,0:T(8,128)S(1)}, f32[32,128]{1,0:T(8,128)S(1)}, u32[]{:S(2)}, u32[]{:S(2)}) collective-permute-start(f32[32,128]{1,0:T(8,128)S(1)} %apply.4.vec_0.vec_2), channel_id=1, source_target_pairs={{0,1},{1,2},{2,3},{3,4},{4,5},{5,6},{6,7},{7,8},{8,9},{9,10},{10,1... | collective-permute-start | bytes 49160 | tf_op jit(solution)/shard_map/ppermute | solution.py:515
  149.1 5.1 %collective-permute-start.9 = (f32[32,128]{1,0:T(8,128)S(1)}, f32[32,128]{1,0:T(8,128)S(1)}, u32[]{:S(2)}, u32[]{:S(2)}) collective-permute-start(f32[32,128]{1,0:T(8,128)S(1)} %apply.4.vec_0.vec_2), channel_id=1, source_target_pairs={{1,0},{2,1},{3,2},{4,3},{5,4},{6,5},{7,6},{8,7},{9,8},{10,9},{11,1... | collective-permute-start | bytes 49160 | tf_op jit(solution)/shard_map/ppermute | solution.py:515
  265.0 1.5 copy-start
  266.6 3.7 %copy-start.2 = (f32[2,65536]{1,0:T(2,128)S(1)}, f32[2,65536]{1,0:T(2,128)}, u32[]{:S(2)}) copy-start(f32[2,65536]{1,0:T(2,128)} %coords_ref.1) | copy-start | bytes 1572868
  266.6 3.7 %copy-start.3 = (f32[2,2048]{1,0:T(2,128)S(1)}, f32[2,2048]{1,0:T(2,128)}, u32[]{:S(2)}) copy-start(f32[2,2048]{1,0:T(2,128)} %right_ref.1) | copy-start | bytes 49156
  266.6 3.7 %copy-start.4 = (f32[2048]{0:T(1024)S(1)}, f32[2048]{0:T(1024)}, u32[]{:S(2)}) copy-start(f32[2048]{0:T(1024)} %param.14) | copy-start | bytes 24580
  266.6 3.7 %copy-start.5 = (s32[1,5,3]{1,0,2:T(1,128)S(1)}, s32[1,5,3]{1,0,2:T(1,128)}, u32[]{:S(2)}) copy-start(s32[1,5,3]{1,0,2:T(1,128)} %param.17) | copy-start | bytes 184
Sparse Core Ops, SparseCore 0:
  16.0 76.9 all-gather.10
  190.4 74.6 all-gather.12

commit v3 on v0

--- a/solution.py
+++ b/solution.py
@@ -1,9 +1,27 @@
+import functools
+
 import jax
 import jax.numpy as jnp
 from jax import lax
+from jax.experimental import pallas as pl
+from jax.experimental.pallas import tpu as pltpu
 from jax.sharding import PartitionSpec as P
 
 ITERS = 3
+LANES = 128
+SCALE = 4.0**0.2
+HEAD = 5.0 / SCALE**4
+FAR = 1e18
+PAIRS = [(i, j) for i in range(ITERS + 1) for j in range(i, ITERS + 1)]
+OK_ROW = 2 * len(PAIRS)
+MADE = OK_ROW + 1
+SUM_ROWS = 16
+GUARD = 3e-5
+KEPT = 136
+MOST = 3.0
+SMEM = pltpu.MemorySpace.SMEM
+VMEM = pltpu.MemorySpace.VMEM
+TILE = ("far", "near")
 
 
 def padded(array, sides, width):
@@ -32,8 +50,8 @@
     return lax.optimization_barrier(values.astype(jnp.bfloat16)).astype(jnp.float32)
 
 
-def body(right_side, noise_var, coords, counts, pair_list):
-    tile_count = lax.axis_size("tile")
+def any_graph(right_side, noise_var, coords, counts, pair_list):
+    tile_count = lax.axis_size(TILE)
     tile_len = right_side.shape[1]
     columns = right_side.shape[0]
     row_block = min(512, tile_len)
@@ -47,13 +65,10 @@
         city_shift = (pair_kind == 2).astype(jnp.int32) - (pair_kind == 3).astype(jnp.int32)
         return second_tile + tile_count * (1 + city_shift)
 
-    residual = right_side * valid_mask[None, :]
-    direction = residual
-    solution_field = jnp.zeros_like(residual)
-    norm_now = lax.psum(jnp.sum(residual * residual, axis=1), ("city", "tile"))
-    for iteration in range(ITERS):
+    def iterate(carry, _):
+        residual, direction, solution_field, norm_now = carry
         own_dirs = direction.astype(jnp.bfloat16)
-        city_dirs = lax.all_gather(own_dirs[None], "tile", axis=0, tiled=True)
+        city_dirs = lax.all_gather(own_dirs[None], TILE, axis=0, tiled=True)
         wide_dirs = padded(city_dirs, (("city", 0),), tile_count)
 
         def add_pair(slot_id, buffer):
@@ -105,34 +120,652 @@
             0, slot_count, add_pair, jnp.zeros((tile_count, columns, tile_len), jnp.float32)
         )
         arrived = lax.all_to_all(
-            buffer.astype(jnp.bfloat16), "tile", split_axis=0, concat_axis=0, tiled=True
+            buffer.astype(jnp.bfloat16), TILE, split_axis=0, concat_axis=0, tiled=True
         ).astype(buffer.dtype)
         summed = jnp.sum(arrived, axis=0)
         applied = valid_mask[None, :] * summed + noise_eff[None, :] * direction
-        curvature = lax.psum(jnp.sum(direction * applied, axis=1), ("city", "tile"))
+        curvature = lax.psum(jnp.sum(direction * applied, axis=1), ("city", *TILE))
         step_size = norm_now / curvature
         solution_field = solution_field + step_size[:, None] * direction
         residual = residual - step_size[:, None] * applied
+        norm_next = lax.psum(jnp.sum(residual * residual, axis=1), ("city", *TILE))
+        direction = residual + (norm_next / norm_now)[:, None] * direction
+        return (residual, direction, solution_field, norm_next), None
+
+    residual = right_side * valid_mask[None, :]
+    norm_now = lax.psum(jnp.sum(residual * residual, axis=1), ("city", *TILE))
+    carry = (residual, residual, jnp.zeros_like(residual), norm_now)
+    (residual, _, solution_field, _), _ = lax.scan(iterate, carry, None, length=ITERS)
+    return (solution_field, residual)
+
+
+def folded(ref, row):
+    length = ref.shape[1]
+    return jnp.concatenate(
+        [ref[row : row + 1, left : left + LANES] for left in range(0, length, LANES)], axis=0
+    )
+
+
+def columns_of(rows):
+    missing = LANES - rows.shape[0]
+    return jnp.transpose(jnp.concatenate([rows, jnp.zeros((missing, LANES), rows.dtype)], axis=0))
+
+
+def spread(rows, ref):
+    turned = columns_of(rows)
+    for c in range(rows.shape[0]):
+        ref[c * LANES : (c + 1) * LANES, :] = jnp.broadcast_to(
+            turned[:, c : c + 1], (LANES, LANES)
+        )
+
+
+def taken(values, source):
+    chunk, lane = source // LANES, source % LANES
+    result = jnp.zeros_like(values)
+    for c in range(values.shape[0]):
+        row = jnp.broadcast_to(values[c : c + 1, :], values.shape)
+        result = jnp.where(chunk == c, jnp.take_along_axis(row, lane, axis=1), result)
+    return result
+
+
+def pack_kernel(place, table, right_ref, noise_ref, out_ref):
+    chunks = right_ref.shape[1] // LANES
+    lane = lax.broadcasted_iota(jnp.int32, (chunks, LANES), 1)
+    valid = lax.broadcasted_iota(jnp.int32, (chunks, LANES), 0) * LANES + lane < place[0]
+    rows = [jnp.where(valid, folded(right_ref, r), 0.0) for r in range(2)]
+    rows.append(jnp.where(valid, folded(noise_ref, 0), -1.0))
+    entries = jnp.zeros((chunks, LANES), jnp.int32)
+    for k in range(table.shape[0]):
+        entries = jnp.where(lane == k, table[k], entries)
+    rows.append(entries.astype(jnp.float32))
+    out_ref[...] = jnp.concatenate(rows, axis=0).astype(jnp.bfloat16)
+
+
+def arrange(mine, coords_ref, out_ref, rank_ref):
+    length = coords_ref.shape[1]
+    chunks = length // LANES
+    lane = lax.broadcasted_iota(jnp.int32, (chunks, LANES), 1)
+    index = lax.broadcasted_iota(jnp.int32, (chunks, LANES), 0) * LANES + lane
+    x, y = folded(coords_ref, 0), folded(coords_ref, 1)
+    packed = mine[...].astype(jnp.float32)
+    right = [packed[r * chunks : (r + 1) * chunks, :] for r in range(2)]
+    noise = packed[2 * chunks : 3 * chunks, :]
+    valid = noise >= 0.0
+
+    least = jnp.min(jnp.where(valid, y, FAR), keepdims=True)
+    most = jnp.max(jnp.where(valid, y, -FAR), keepdims=True)
+    top = float(LANES - 2)
+    level = jnp.floor((y - least) * (top / jnp.maximum(most - least, 1e-6)))
+    level = jnp.where(valid, jnp.clip(level, 0.0, top), top + 1.0)
+    down = lax.broadcasted_iota(jnp.int32, (LANES, LANES), 0)
+    along = lax.broadcasted_iota(jnp.int32, (LANES, LANES), 1)
+
+    def dot(a, b, dims=((1,), (0,))):
+        return lax.dot_general(
+            a.astype(jnp.bfloat16),
+            b.astype(jnp.bfloat16),
+            (dims, ((), ())),
+            preferred_element_type=jnp.float32,
+        )
+
+    def one_hot(rows, c):
+        return jnp.where(down.astype(jnp.float32) == rows[c : c + 1, :], 1.0, 0.0)
+
+    ones = jnp.ones((LANES, LANES), jnp.float32)
+    counter = jnp.concatenate([jnp.where(down < along, 1.0, 0.0), ones], axis=1)
+    running = jnp.zeros((LANES, LANES), jnp.float32)
+    ahead = []
+    for c in range(chunks):
+        counted = dot(one_hot(level, c), counter)
+        ahead.append(counted[:, 0:LANES] + running)
+        running = running + counted[:, LANES:]
+    tens = jnp.floor(running * (1.0 / 64.0))
+    below = jnp.where(along < down, 1.0, 0.0)
+    base = 64.0 * dot(below, tens) + dot(below, running - 64.0 * tens)
+    rank = jnp.concatenate(
+        [
+            jnp.sum(one_hot(level, c) * (ahead[c] + base), axis=0, keepdims=True)
+            for c in range(chunks)
+        ],
+        axis=0,
+    ).astype(jnp.int32)
+    rank_ref[...] = rank
+    row_of, lane_of = rank // LANES, (rank % LANES).astype(jnp.float32)
+    first = lax.broadcasted_iota(jnp.int32, (chunks, LANES), 0)
+    lanes = lane.astype(jnp.float32)
+    found = jnp.zeros((2 * chunks, LANES), jnp.float32)
+    for c in range(chunks):
+        there = first == row_of[c : c + 1, :]
+        values = jnp.concatenate(
+            [jnp.where(there, lanes, 0.0), jnp.where(there, float(c), 0.0)], axis=0
+        )
+        found = found + dot(values, one_hot(lane_of, c), ((1,), (1,)))
+    source = (found[0:chunks, :] + LANES * found[chunks:, :]).astype(jnp.int32)
+    for place_of, rows in enumerate((x, y, right[0], right[1], noise)):
+        out_ref[place_of * chunks : (place_of + 1) * chunks, :] = taken(rows, source)
+
+
+def order_kernel(
+    own, table, gathered, coords, out_ref, rank_ref, info, links, degree, order, mine, points, sems
+):
+    tiles = table.shape[0]
+    near = gathered.shape[0]
+    length = points.shape[1]
+    for t in range(tiles):
+        degree[t] = 0
+        links[2 * t] = -1
+        links[2 * t + 1] = -1
+    info[1] = 0
+
+    def join(a, b):
+        count = degree[a]
+        links[2 * a + jnp.minimum(count, 1)] = b
+        degree[a] = count + 1
+
+    def read(t, carry):
+        selfs, edges, to_next, to_prev = carry
+        for slot in range(table.shape[1] // 3):
+            a, b, kind = table[t, 3 * slot], table[t, 3 * slot + 1], table[t, 3 * slot + 2]
+            pair = (kind == 1) & (a != b)
+            selfs = selfs + ((kind == 1) & (a == b)).astype(jnp.int32)
+            edges = edges + pair.astype(jnp.int32)
+            to_next = jnp.where(kind == 2, a, to_next)
+            to_prev = jnp.where(kind == 3, a, to_prev)
+
+            @pl.when(pair)
+            def _():
+                join(a, b)
+                join(b, a)
+
+        return selfs, edges, to_next, to_prev
+
+    zero, none = jnp.int32(0), jnp.int32(-1)
+    found = lax.fori_loop(0, tiles, read, (zero, zero, none, none))
+    selfs, edges, to_next, to_prev = found
+
+    def end_of(t, best):
+        fits = (degree[t] <= 1) & (t != to_next) & (best < 0)
+        return jnp.where(fits, t, best)
+
+    start = lax.fori_loop(0, tiles, end_of, to_prev)
+    complete = (start >= 0) & (selfs == tiles) & (edges == tiles - 1)
+
+    def walk(p, carry):
+        before, tile, good = carry
+        order[p] = tile
+        good = good & (degree[tile] <= 2)
+
+        @pl.when(tile == own[0])
+        def _():
+            info[1] = p
+
+        a, b = links[2 * tile], links[2 * tile + 1]
+        following = jnp.where(a != before, a, b)
+        good = good & ((following >= 0) | (p == tiles - 1))
+        return tile, jnp.maximum(following, 0), good
+
+    first = jnp.maximum(start, 0)
+    _, _, good = lax.fori_loop(0, tiles, walk, (jnp.int32(-1), first, complete))
+    last = order[tiles - 1]
+    good = good & ((to_prev < 0) | (degree[first] <= 1)) & (degree[last] <= 1)
+    good = good & ((to_next < 0) | (last == to_next))
+    tile = order[own[0]]
+    info[0] = tile
+    info[2] = good.astype(jnp.int32)
+    info[3] = ((own[0] > 0) | (to_prev >= 0)).astype(jnp.int32)
+    info[4] = ((own[0] < tiles - 1) | (to_next >= 0)).astype(jnp.int32)
+    start_of = pl.multiple_of(tile * length, length)
+    copies = [
+        pltpu.make_async_copy(gathered.at[tile % near, tile // near], mine, sems.at[0]),
+        pltpu.make_async_copy(coords.at[:, pl.ds(start_of, length)], points, sems.at[1]),
+    ]
+    for copy in copies:
+        copy.start()
+    for copy in copies:
+        copy.wait()
+    arrange(mine, points, out_ref, rank_ref)
+
+
+def close_chunks(mine, before, after, info, bounds, far):
+    chunks = far.shape[1] // 2
+    origin_x, origin_y = mine[0:1, 0:1], mine[chunks : chunks + 1, 0:1]
+
+    def box(ref):
+        good = ref[4 * chunks : 5 * chunks, :] >= 0.0
+        sides = []
+        for row in (0, chunks):
+            values = ref[row : row + chunks, :]
+            sides.append(jnp.min(jnp.where(good, values, FAR), axis=1, keepdims=True))
+            sides.append(jnp.max(jnp.where(good, values, -FAR), axis=1, keepdims=True))
+        return sides
+
+    near_box = box(mine)
+    for slot, ref in enumerate((mine, before, after)):
+        far_box = near_box if slot == 0 else box(ref)
+        least = jnp.full((chunks, 1), float(chunks), jnp.float32)
+        most = jnp.zeros((chunks, 1), jnp.float32)
+        for c in range(chunks):
+            f = [side[c : c + 1, :] for side in far_box]
+            gap_x = jnp.maximum(jnp.maximum(near_box[0] - f[1], f[0] - near_box[1]), 0.0)
+            gap_y = jnp.maximum(jnp.maximum(near_box[2] - f[3], f[2] - near_box[3]), 0.0)
+            close = gap_x * gap_x + gap_y * gap_y < 1.0001
+            least = jnp.where(close, jnp.minimum(least, float(c)), least)
+            most = jnp.where(close, float(c + 1), most)
+        pairs = jnp.floor(jnp.maximum(most - least + 1.0, 0.0) * 0.5)
+        least = jnp.minimum(least, chunks - 2.0 * pairs)
+        for c in range(chunks):
+            bounds[slot * chunks + c] = jnp.max(least[c : c + 1, :]).astype(jnp.int32)
+            count = jnp.max(pairs[c : c + 1, :]).astype(jnp.int32)
+            bounds[(3 + slot) * chunks + c] = count if slot == 0 else count * info[2 + slot]
+        far[slot, 0:chunks, :] = (ref[0:chunks, :] - origin_x) * SCALE
+        far[slot, chunks : 2 * chunks, :] = (ref[chunks : 2 * chunks, :] - origin_y) * SCALE
+
+
+def row_sums(bounds, base, mine, vecs, out_ref, block_of):
+    chunks = out_ref.shape[0] // 2
+    groups = LANES // 16
+
+    def near_chunk(i, number):
+        sums = tuple(jnp.zeros((16, LANES), jnp.float32) for _ in range(2 * groups))
+        carry = (number, sums)
+        for slot in range(3):
+
+            def far_chunks(j, carry):
+                number, sums = carry
+                found = list(sums)
+                rows = []
+                start = bounds[slot * chunks + i] + 2 * j
+                for h in range(2):
+                    c = base + start + h
+                    rows.append([vecs[slot][pl.ds(c + r * chunks, 1), :] for r in range(2)])
+                for g, h, value in block_of(number, slot, i, start):
+                    for r in range(2):
+                        found[2 * g + r] = found[2 * g + r] + value * rows[h][r]
+                return number + 1, tuple(found)
+
+            carry = lax.fori_loop(0, bounds[(3 + slot) * chunks + i], far_chunks, carry)
+        number, sums = carry
+        noise = mine[pl.ds(4 * chunks + i, 1), :]
+        for r in range(2):
+            block = jnp.concatenate(sums[r::2], axis=0)
+            total = jnp.sum(jnp.transpose(block), axis=0, keepdims=True)
+            own = vecs[0][pl.ds(base + r * chunks + i, 1), :]
+            out_ref[pl.ds(r * chunks + i, 1), :] = jnp.where(noise >= 0.0, total + noise * own, own)
+        return number
+
+    return lax.fori_loop(0, chunks, near_chunk, jnp.int32(0))
+
+
+def evaluated(near_x, near_y, far, slot, i, start):
+    chunks = far.shape[1] // 2
+    cells = []
+    for h in range(2):
+        c = start + h
+        cells.append((far[slot, pl.ds(c, 1), :], far[slot, pl.ds(chunks + c, 1), :]))
+    for g in range(LANES // 16):
+        here = pl.ds(pl.multiple_of(i * LANES + 16 * g, 16), 16)
+        x, y = near_x[here, :], near_y[here, :]
+        for h, (far_x, far_y) in enumerate(cells):
+            across, along = x - far_x, y - far_y
+            square = jnp.maximum(across * across + along * along, 1e-30)
+            inside = jnp.maximum(SCALE - square * lax.rsqrt(square), 0.0)
+            power = inside * inside
+            yield g, h, power * power * (HEAD - inside)
+
+
+def build_kernel(info, mine, before, after, out_ref, blocks, bounds, far, near_x, near_y):
+    chunks = out_ref.shape[0] // 2
+    close_chunks(mine, before, after, info, bounds, far)
+    spread(far[0, 0:chunks, :], near_x)
+    spread(far[0, chunks : 2 * chunks, :], near_y)
+
+    def block_of(number, slot, i, start):
+        place = jnp.minimum(number, blocks.shape[0] - 1)
+        for g, h, value in evaluated(near_x, near_y, far, slot, i, start):
+            blocks[place, 16 * g : 16 * g + 16, h * LANES : (h + 1) * LANES] = value.astype(
+                jnp.bfloat16
+            )
+            yield g, h, value
+
+    bounds[6 * chunks] = row_sums(
+        bounds, 2 * chunks, mine, (mine, before, after), out_ref, block_of
+    )
+
+
+def apply_kernel(bounds, mine, vec_0, vec_1, vec_2, far, blocks, out_ref, near_x, near_y):
+    chunks = out_ref.shape[0] // 2
+    vecs = (vec_0, vec_1, vec_2)
+    kept = bounds[6 * chunks] <= blocks.shape[0]
+
+    @pl.when(kept)
+    def _():
+        def block_of(number, slot, i, start):
+            for g in range(LANES // 16):
+                for h in range(2):
+                    value = blocks[number, 16 * g : 16 * g + 16, h * LANES : (h + 1) * LANES]
+                    yield g, h, value.astype(jnp.float32)
+
+        row_sums(bounds, 0, mine, vecs, out_ref, block_of)
+
+    @pl.when(jnp.logical_not(kept))
+    def _():
+        spread(far[0, 0:chunks, :], near_x)
+        spread(far[0, chunks : 2 * chunks, :], near_y)
+
+        def block_of(number, slot, i, start):
+            yield from evaluated(near_x, near_y, far, slot, i, start)
+
+        row_sums(bounds, 0, mine, vecs, out_ref, block_of)
+
+
+def sums_kernel(info, mine, vec_1, vec_2, vec_3, out_ref):
+    chunks = vec_1.shape[0] // 2
+    vecs = (mine[2 * chunks : 4 * chunks, :], vec_1[...], vec_2[...], vec_3[...])
+    rows = []
+    for r in range(2):
+        half = [v[r * chunks : (r + 1) * chunks, :] for v in vecs]
+        rows += [jnp.sum(half[i] * half[j], axis=0, keepdims=True) for i, j in PAIRS]
+    rows.append(jnp.full((1, LANES), 1.0 / LANES, jnp.float32) * info[2].astype(jnp.float32))
+    rows.append(jnp.zeros((LANES - len(rows), LANES), jnp.float32))
+    turned = jnp.transpose(jnp.concatenate(rows, axis=0))
+    out_ref[...] = jnp.broadcast_to(jnp.sum(turned, axis=0, keepdims=True), out_ref.shape)
+
+
+def iterated(gram):
+    def form(a, b):
+        terms = [a[i] * b[j] * gram[i, j] for i in a for j in b]
+        value, size = terms[0], jnp.abs(terms[0])
+        for term in terms[1:]:
+            value, size = value + term, size + jnp.abs(term)
+        return value, value > GUARD * size
+
+    def plus(a, scale, b):
+        keys = sorted(set(a) | set(b))
+        return {
+            k: a[k] + scale * b[k] if k in a and k in b else (a[k] if k in a else scale * b[k])
+            for k in keys
+        }
+
+    one = jnp.ones((1, 1), jnp.float32)
+    res, direction, field = {0: one}, {0: one}, {}
+    norm, good = form(res, res)
+    residuals = []
+    for iteration in range(ITERS):
+        image = {k + 1: v for k, v in direction.items()}
+        curve, fine = form(direction, image)
+        good = good & fine
+        step = norm / curve
+        field = plus(field, step, direction)
+        res = plus(res, -step, image)
+        residuals.append(res)
         if iteration + 1 < ITERS:
-            norm_next = lax.psum(jnp.sum(residual * residual, axis=1), ("city", "tile"))
-        if iteration + 1 < ITERS:
-            direction = residual + (norm_next / norm_now)[:, None] * direction
-            norm_now = norm_next
-    return (solution_field, residual)
+            new, fine = form(res, res)
+            good = good & fine
+            direction = plus(res, new / norm, direction)
+            norm = new
+    return field, residuals, good
+
+
+def gram_of(row, r):
+    column = jnp.transpose(jnp.broadcast_to(row, (LANES, LANES)))
+    gram = {}
+    for k, (i, j) in enumerate(PAIRS):
+        at = r * len(PAIRS) + k
+        gram[i, j] = gram[j, i] = column[at : at + 1, 0:1]
+    return gram
+
+
+def basis_kernel(cities, sums_ref, mine, rank, vec_1, vec_2, vec_3, out_ref):
+    chunks = rank.shape[0]
+    row = jnp.sum(sums_ref[...], axis=0)[0:1, :]
+    lane = lax.broadcasted_iota(jnp.int32, (1, LANES), 1)
+    good = row[:, OK_ROW : OK_ROW + 1] == float(cities)
+    places = rank[...]
+    vecs = (None, vec_1, vec_2, vec_3)
+    rows, made = {}, []
+    for r in range(2):
+        _, residuals, fine = iterated(gram_of(row, r))
+        good = good & fine
+        for k, weights in enumerate(residuals):
+            values = mine[(2 + r) * chunks : (3 + r) * chunks, :]
+            for j in range(1, k + 2):
+                values = values + weights[j] * vecs[j][r * chunks : (r + 1) * chunks, :]
+                made.append(weights[j])
+            rows[k, r] = taken(values, places)
+    row = jnp.where(lane == OK_ROW, jnp.where(good, 1.0, 0.0), row)
+    for k, value in enumerate(made):
+        row = jnp.where(lane == MADE + k, value, row)
+    high = row.astype(jnp.bfloat16).astype(jnp.float32)
+    middle = (row - high).astype(jnp.bfloat16).astype(jnp.float32)
+    low = row - high - middle
+    parts = [rows[k, r] for k in range(ITERS) for r in range(2)]
+    parts += [high, middle, low, jnp.zeros((SUM_ROWS - 3, LANES), jnp.float32)]
+    out_ref[...] = jnp.concatenate(parts, axis=0).astype(jnp.bfloat16)
+
+
+def home_kernel(info, back_ref, sums_ref, packed, field_ref, residual_ref, ok_ref):
+    chunks = field_ref.shape[1] // LANES
+    near, groups = sums_ref.shape[:2]
+    tiles = near * groups
+    terms = sums_ref[...].astype(jnp.float32).reshape(tiles, SUM_ROWS, LANES)
+    terms = terms[:, 0, :] + terms[:, 1, :] + terms[:, 2, :]
+    row = jnp.sum(terms, axis=0, keepdims=True)
+    slot = info[1] % near * groups + info[1] // near
+    here = lax.broadcasted_iota(jnp.int32, (tiles, 1), 0) == slot
+    good = row[:, OK_ROW : OK_ROW + 1] == float(tiles)
+    values = back_ref[0, 0].astype(jnp.float32)
+    start = packed[...].astype(jnp.float32)
+    count = len(PAIRS) - ITERS - 1
+    for r in range(2):
+        field, residuals, fine = iterated(gram_of(row, r))
+        good = good & fine
+        made, at = {}, MADE + r * count
+        for k in range(1, ITERS + 1):
+            made[k, 0] = 1.0
+            for j in range(1, k + 1):
+                made[k, j] = terms[:, at : at + 1]
+                at += 1
+        for ref, weights in ((field_ref, field), (residual_ref, residuals[-1])):
+            left = dict(weights)
+            result = None
+            for k in range(ITERS, 0, -1):
+                if k not in left:
+                    continue
+                share = left[k] / made[k, k]
+                for j in range(k):
+                    left[j] = left[j] - share * made[k, j]
+                if ref is residual_ref:
+                    fine = jnp.min(jnp.where(jnp.abs(share) <= MOST, 1.0, 0.0), keepdims=True)
+                    good = good & (fine > 0.0)
+                weight = jnp.sum(jnp.where(here, share, 0.0), axis=0, keepdims=True)
+                place = (2 * (k - 1) + r) * chunks
+                term = weight * values[place : place + chunks, :]
+                result = term if result is None else result + term
+            weight = jnp.sum(jnp.where(here, left[0], 0.0), axis=0, keepdims=True)
+            result = result + weight * start[r * chunks : (r + 1) * chunks, :]
+            for c in range(chunks):
+                ref[r : r + 1, c * LANES : (c + 1) * LANES] = result[c : c + 1, :]
+    ok_ref[0] = jnp.max(jnp.where(good, 1.0, 0.0)).astype(jnp.int32)
+
+
+def tile_gather(block):
+    return lax.all_gather(lax.all_gather(block, "far"), "near")
+
+
+def whole(shape):
+    return pl.BlockSpec(shape, lambda i, *_: (0,) * len(shape))
+
+
+def params(mib=16):
+    return pltpu.CompilerParams(vmem_limit_bytes=mib * 1024 * 1024)
+
+
+def body(right_side, noise_var, coords, counts, pair_list):
+    own = lax.axis_index(TILE).astype(jnp.int32)
+    tiles, cities = lax.axis_size(TILE), lax.axis_size("city")
+    length = right_side.shape[1]
+    chunks = length // LANES
+    rows = 5 * chunks
+    table = pair_list.reshape(-1)
+    entries = table.shape[0]
+    f32 = functools.partial(jax.ShapeDtypeStruct, dtype=jnp.float32)
+
+    packed = pl.pallas_call(
+        pack_kernel,
+        grid_spec=pltpu.PrefetchScalarGridSpec(
+            num_scalar_prefetch=2,
+            grid=(1,),
+            in_specs=[whole((2, length)), whole((1, length))],
+            out_specs=whole((4 * chunks, LANES)),
+        ),
+        out_shape=jax.ShapeDtypeStruct((4 * chunks, LANES), jnp.bfloat16),
+        compiler_params=params(),
+        name="pack",
+    )(counts, table, right_side, noise_var[None, :])
+
+    gathered = tile_gather(packed)
+    city_table = gathered[:, :, 3 * chunks, :entries].astype(jnp.int32).reshape(tiles, entries)
+    mine, rank, info = pl.pallas_call(
+        order_kernel,
+        in_specs=[
+            pl.BlockSpec(memory_space=SMEM),
+            pl.BlockSpec(memory_space=SMEM),
+            pl.BlockSpec(memory_space=pl.ANY),
+            pl.BlockSpec(memory_space=pl.ANY),
+        ],
+        out_specs=[
+            pl.BlockSpec(memory_space=VMEM),
+            pl.BlockSpec(memory_space=VMEM),
+            pl.BlockSpec(memory_space=SMEM),
+        ],
+        out_shape=[
+            f32((rows, LANES)),
+            jax.ShapeDtypeStruct((chunks, LANES), jnp.int32),
+            jax.ShapeDtypeStruct((8,), jnp.int32),
+        ],
+        scratch_shapes=[
+            pltpu.SMEM((2 * tiles,), jnp.int32),
+            pltpu.SMEM((tiles,), jnp.int32),
+            pltpu.SMEM((tiles,), jnp.int32),
+            pltpu.VMEM((4 * chunks, LANES), jnp.bfloat16),
+            pltpu.VMEM((2, length), jnp.float32),
+            pltpu.SemaphoreType.DMA((2,)),
+        ],
+        compiler_params=params(),
+        name="order",
+    )(own[None], city_table, gathered, coords)
+
+    forward = [(i, i + 1) for i in range(tiles * cities - 1)]
+    backward = [(j, i) for i, j in forward]
+
+    def neighbours(block):
+        axes = ("city", *TILE)
+        return lax.ppermute(block, axes, forward), lax.ppermute(block, axes, backward)
+
+    in_vmem = pl.BlockSpec(memory_space=VMEM)
+    in_smem = pl.BlockSpec(memory_space=SMEM)
+    spread_scratch = [pltpu.VMEM((length, LANES), jnp.float32)] * 2
+    before, after = neighbours(mine)
+    vec_1, blocks, bounds, far = pl.pallas_call(
+        build_kernel,
+        in_specs=[in_smem] + [in_vmem] * 3,
+        out_specs=[in_vmem, in_vmem, in_smem, in_vmem],
+        out_shape=[
+            f32((2 * chunks, LANES)),
+            pltpu.VMEM((KEPT, LANES, 2 * LANES), jnp.bfloat16),
+            jax.ShapeDtypeStruct((6 * chunks + 1,), jnp.int32),
+            f32((3, 2 * chunks, LANES)),
+        ],
+        scratch_shapes=spread_scratch,
+        compiler_params=params(),
+        name="build",
+    )(info, mine, before, after)
+    blocks = pltpu.with_memory_space_constraint(blocks, VMEM)
+
+    def apply(vec):
+        before, after = neighbours(vec)
+        return pl.pallas_call(
+            apply_kernel,
+            in_specs=[in_smem] + [in_vmem] * 6,
+            out_specs=in_vmem,
+            out_shape=f32((2 * chunks, LANES)),
+            scratch_shapes=spread_scratch,
+            compiler_params=params(),
+            name="apply",
+        )(bounds, mine, vec, before, after, far, blocks)
+
+    vec_2 = apply(vec_1)
+    vec_3 = apply(vec_2)
+
+    sums = pl.pallas_call(
+        sums_kernel,
+        grid_spec=pltpu.PrefetchScalarGridSpec(
+            num_scalar_prefetch=1,
+            grid=(1,),
+            in_specs=[whole((rows, LANES))] + [whole((2 * chunks, LANES))] * 3,
+            out_specs=whole((8, LANES)),
+        ),
+        out_shape=f32((8, LANES)),
+        compiler_params=params(),
+        name="sums",
+    )(info, mine, vec_1, vec_2, vec_3)
+    size = 6 * chunks + SUM_ROWS
+    basis = pl.pallas_call(
+        functools.partial(basis_kernel, cities),
+        out_shape=jax.ShapeDtypeStruct((size, LANES), jnp.bfloat16),
+        compiler_params=params(),
+        name="basis",
+    )(lax.all_gather(sums, "city"), mine, rank, vec_1, vec_2, vec_3)
+    back = tile_gather(basis)
+    near, groups = back.shape[:2]
+    field, residual, good = pl.pallas_call(
+        home_kernel,
+        grid_spec=pltpu.PrefetchScalarGridSpec(
+            num_scalar_prefetch=1,
+            grid=(1,),
+            in_specs=[
+                pl.BlockSpec(
+                    (1, 1, size, LANES), lambda i, info: (info[1] % near, info[1] // near, 0, 0)
+                ),
+                pl.BlockSpec(
+                    (near, groups, SUM_ROWS, LANES),
+                    lambda i, info: (0, 0, 6 * chunks // SUM_ROWS, 0),
+                ),
+                whole((4 * chunks, LANES)),
+            ],
+            out_specs=[whole((2, length)), whole((2, length)), pl.BlockSpec(memory_space=SMEM)],
+        ),
+        out_shape=[f32((2, length)), f32((2, length)), jax.ShapeDtypeStruct((1,), jnp.int32)],
+        compiler_params=params(),
+        name="home",
+    )(info, back, back, packed)
+    return lax.cond(
+        good[0] > 0,
+        lambda *args: (field, residual),
+        any_graph,
+        right_side,
+        noise_var,
+        coords,
+        counts,
+        pair_list,
+    )
 
 
 def solution(mesh):
+    cities, tiles = mesh.devices.shape
+    groups = 4 if tiles % 8 == 0 else 2
+    mesh = jax.sharding.Mesh(mesh.devices.reshape(cities, groups, tiles // groups), ("city", *TILE))
     placed = (
-        P(None, ("city", "tile")),
-        P(("city", "tile")),
+        P(None, ("city", *TILE)),
+        P(("city", *TILE)),
         P(None, "city"),
-        P(("city", "tile")),
-        P(("city", "tile"), None, None),
+        P(("city", *TILE)),
+        P(("city", *TILE), None, None),
     )
     return jax.shard_map(
         body,
         mesh=mesh,
         in_specs=placed,
-        out_specs=(P(None, ("city", "tile")), P(None, ("city", "tile"))),
+        out_specs=(P(None, ("city", *TILE)), P(None, ("city", *TILE))),
         check_vma=False,
     )

time: 1250 us -> 177 us (0.14); the launches traced: 1240 us -> 176 us
  blocking collectives: 837 us -> 121 us
  matrix products: 136 us -> 0 us
  starting transfers between devices: 111 us -> 16.8 us
  loops' own time: 70.6 us -> 0.23 us
  waiting for transfers between devices: 53 us -> 2.7 us
  Pallas kernels: 0 us -> 31.9 us
  local copies, waits for them, and re-layouts: 18.8 us -> 0.87 us
    psum x5 -> x0, blocking collectives: 514 us -> none  [the longest x2 209 us: body(): curvature = lax.psum(jnp.sum(direction * applied, axis=1), ('city', 'tile'))]
    all_to_all x2 -> x0, blocking collectives: 227 us -> none  [body(): lax.all_to_all(buffer.astype(jnp.bfloat16), 'tile', split_axis=0, concat_...]
    dot_general x48 -> x0, matrix products: 136 us -> none  [the longest x24 67.9 us: compute(): lax.dot_general(far_vec, kernel, (((1,), (1,)), ((), ())), preferred_elem...]
    all_to_all x1 -> x0, starting transfers between devices: 92.8 us -> none  [body(): lax.all_to_all(buffer.astype(jnp.bfloat16), 'tile', split_axis=0, concat_...]
    another operation x18 -> x1, loops' own time: 70.6 us -> 0.23 us  [body(): lax.cond(good[0] > 0, lambda *args: (field, residual), any_graph, right_s...]
    pallas_call x0 -> x8, Pallas kernels: none -> 31.9 us  [the longest x1 11.4 us: body(): pl.pallas_call(build_kernel, in_specs=[in_smem] + [in_vmem] * 3, out_spec...]
    ppermute x8 -> x6, waiting for transfers between devices: 31 us -> 2.7 us  [the longest x3 2.69 us: neighbours(): lax.ppermute(block, axes, forward)]
    all_gather x3 -> x5, blocking collectives: 96 us -> 121 us  [the longest x4 88 us: tile_gather(): return lax.all_gather(lax.all_gather(block, 'far'), 'near')]
  transfers between devices with their start and end apart: 9 -> 6, of which waited for: 8 -> 3; matrix products, arithmetic and copies ran while one was open for 0% -> 0% of each run, Pallas kernels for 0% -> 0%
where the time goes in v3:
time: 177 us; the launch traced here: 176 us
  blocking collectives  121 us (68%)
  Pallas kernels  31.9 us (18%)
  starting transfers between devices  16.8 us (9%)
  waiting for transfers between devices  2.7 us (2%)
  between operations  2.29 us (1%)
    all_gather x4, blocking collectives, tile_gather(): return lax.all_gather(lax.all_gather(block, 'far'), 'near')  88 us
    all_gather x1, blocking collectives, body(): lax.all_gather(sums, 'city')  33.5 us
    pallas_call x1, Pallas kernels, body(): pl.pallas_call(build_kernel, in_specs=[in_smem] + [in_vmem] * 3, out_spec...  11.4 us
    ppermute x3, starting transfers between devices, neighbours(): lax.ppermute(block, axes, forward)  10.9 us
    pallas_call x2, Pallas kernels, apply(): pl.pallas_call(apply_kernel, in_specs=[in_smem] + [in_vmem] * 6, out_spec...  9.86 us
    pallas_call x1, Pallas kernels, body(): pl.pallas_call(order_kernel, in_specs=[pl.BlockSpec(memory_space=SMEM), p...  6.79 us
    ppermute x3, starting transfers between devices, neighbours(): lax.ppermute(block, axes, backward)  5.91 us
  transfers between devices with their start and end apart: 6, of which 3 were waited for; matrix products, arithmetic and copies ran while one was open for 0% of the time, Pallas kernels for 0%

profile of v3, /device:TPU:1, one launch (start us, length us, event | category | flops | bytes accessed | tf_op | source)
XLA Modules:
  0.0 176.3 jit_solution(15210915406658838198)
XLA Ops:
  1.3 0.8 copy.14
  2.1 0.1 reshape.38.table
  2.1 1.3 pack.1.packed
  3.4 23.7 %all-gather.1 = bf16[256,128]{1,0:T(8,128)(2,1)S(1)} all-gather(bf16[64,128]{1,0:T(8,128)(2,1)S(1)} %pack.1.packed), channel_id=3, replica_groups=mesh['city'=16,'far'=4,'near'=8] {'far'}, dimensions={0}, use_global_device_ids=true | all-gather | bytes 81920 | tf_op jit(solution)/shard_map/all_gather | solution.py:592
  27.1 18.2 %all-gather.2 = bf16[32,64,128]{2,1,0:T(8,128)(2,1)S(1)} all-gather(bf16[4,64,128]{2,1,0:T(8,128)(2,1)S(1)} %bitcast.94), channel_id=4, replica_groups=mesh['city'=16,'far'=4,'near'=8] {'near'}, dimensions={0}, use_global_device_ids=true | all-gather | bytes 589824 | tf_op jit(solution)/shard_map/all_gather | solution.py:592
  45.3 6.8 %order.1 = (f32[80,128]{1,0:T(8,128)S(1)}, s32[16,128]{1,0:T(8,128)S(1)}, s32[8]{0:T(128)S(1)}) custom-call(s32[1]{0:T(128)} %bitcast.21.own, s32[32,15]{1,0:T(8,128)S(1)} %bitcast.60, bf16[8,4,64,128]{3,2,1,0:T(8,128)(2,1)S(1)} %bitcast.58, f32[2,65536]{1,0:T(2,128)} %coords.1), custom_call_target="tpu_custom_call" | custom-call | tf_op jit(solution)/shard_map/order/pallas_call | solution.py:628
  52.1 2.1 %collective-permute-start.5 = (f32[80,128]{1,0:T(8,128)S(1)}, f32[80,128]{1,0:T(8,128)S(1)}, u32[]{:S(2)}, u32[]{:S(2)}) collective-permute-start(f32[80,128]{1,0:T(8,128)S(1)} %get-tuple-element.275.mine), channel_id=1, source_target_pairs={{1,0},{2,1},{3,2},{4,3},{5,4},{6,5},{7,6},{8,7},{9,8},{10,9},{11,1... | collective-permute-start | bytes 122888 | tf_op jit(solution)/shard_map/ppermute | solution.py:663
  54.2 3.5 %collective-permute-start.4 = (f32[80,128]{1,0:T(8,128)S(1)}, f32[80,128]{1,0:T(8,128)S(1)}, u32[]{:S(2)}, u32[]{:S(2)}) collective-permute-start(f32[80,128]{1,0:T(8,128)S(1)} %get-tuple-element.275.mine), channel_id=1, source_target_pairs={{0,1},{1,2},{2,3},{3,4},{4,5},{5,6},{6,7},{7,8},{8,9},{9,10},{10,1... | collective-permute-start | bytes 122888 | tf_op jit(solution)/shard_map/ppermute | solution.py:663
  57.7 0.0 collective-permute-done.5.after
  57.7 1.1 collective-permute-done.4.before
  58.8 11.4 %build.1 = (f32[32,128]{1,0:T(8,128)S(1)}, bf16[136,128,256]{2,1,0:T(8,128)(2,1)S(1)}, s32[97]{0:T(128)S(1)}, f32[3,32,128]{2,1,0:T(8,128)S(1)}) custom-call(s32[8]{0:T(128)S(1)} %get-tuple-element.274.info, f32[80,128]{1,0:T(8,128)S(1)} %get-tuple-element.275.mine, f32[80,128]{1,0:T(8,128)S(1)} %collective-permute-done.4.before, ...), custom_call_target="tpu_custom_call" | custom-call | tf_op jit(solution)/shard_map/build/pallas_call | solution.py:669
  70.2 1.9 %collective-permute-start.7 = (f32[32,128]{1,0:T(8,128)S(1)}, f32[32,128]{1,0:T(8,128)S(1)}, u32[]{:S(2)}, u32[]{:S(2)}) collective-permute-start(f32[32,128]{1,0:T(8,128)S(1)} %get-tuple-element.276.vec_0.vec_1), channel_id=1, source_target_pairs={{1,0},{2,1},{3,2},{4,3},{5,4},{6,5},{7,6},{8,7},{9,8},{10,9},{11,1... | collective-permute-start | bytes 49160 | tf_op jit(solution)/shard_map/ppermute | solution.py:663
  72.1 3.6 %collective-permute-start.6 = (f32[32,128]{1,0:T(8,128)S(1)}, f32[32,128]{1,0:T(8,128)S(1)}, u32[]{:S(2)}, u32[]{:S(2)}) collective-permute-start(f32[32,128]{1,0:T(8,128)S(1)} %get-tuple-element.276.vec_0.vec_1), channel_id=1, source_target_pairs={{0,1},{1,2},{2,3},{3,4},{4,5},{5,6},{6,7},{7,8},{8,9},{9,10},{10,1... | collective-permute-start | bytes 49160 | tf_op jit(solution)/shard_map/ppermute | solution.py:663
  75.7 0.0 collective-permute-done.7.vec_2
  75.7 0.8 collective-permute-done.6.vec_1
  76.6 4.9 %apply.2.vec_0.vec_2 = f32[32,128]{1,0:T(8,128)S(1)} custom-call(s32[97]{0:T(128)S(1)} %get-tuple-element.277.bounds, f32[80,128]{1,0:T(8,128)S(1)} %get-tuple-element.275.mine, f32[32,128]{1,0:T(8,128)S(1)} %get-tuple-element.276.vec_0.vec_1, f32[32,128]{1,0:T(8,128)S(1)} %collective-permute-done.6.vec_1, f32[32,128]{1,0:T(8,128)S(1)} %collective-permute-done.7.vec_2, ...), custom_call_target="tpu_custom_call" | custom-call | tf_op jit(solution)/shard_map/apply/pallas_call | solution.py:687
  81.5 1.9 %collective-permute-start.9 = (f32[32,128]{1,0:T(8,128)S(1)}, f32[32,128]{1,0:T(8,128)S(1)}, u32[]{:S(2)}, u32[]{:S(2)}) collective-permute-start(f32[32,128]{1,0:T(8,128)S(1)} %apply.2.vec_0.vec_2), channel_id=1, source_target_pairs={{1,0},{2,1},{3,2},{4,3},{5,4},{6,5},{7,6},{8,7},{9,8},{10,9},{11,1... | collective-permute-start | bytes 49160 | tf_op jit(solution)/shard_map/ppermute | solution.py:663
  83.5 3.7 %collective-permute-start.8 = (f32[32,128]{1,0:T(8,128)S(1)}, f32[32,128]{1,0:T(8,128)S(1)}, u32[]{:S(2)}, u32[]{:S(2)}) collective-permute-start(f32[32,128]{1,0:T(8,128)S(1)} %apply.2.vec_0.vec_2), channel_id=1, source_target_pairs={{0,1},{1,2},{2,3},{3,4},{4,5},{5,6},{6,7},{7,8},{8,9},{9,10},{10,1... | collective-permute-start | bytes 49160 | tf_op jit(solution)/shard_map/ppermute | solution.py:663
  87.2 0.0 copy-start
  87.2 0.0 copy-start.1
  87.2 0.0 copy-start.2
  87.2 0.0 copy-start.3
  87.3 0.0 collective-permute-done.9.vec_2
  87.3 0.8 collective-permute-done.8.vec_1
  88.1 4.9 %apply.3.vec_3 = f32[32,128]{1,0:T(8,128)S(1)} custom-call(s32[97]{0:T(128)S(1)} %get-tuple-element.277.bounds, f32[80,128]{1,0:T(8,128)S(1)} %get-tuple-element.275.mine, f32[32,128]{1,0:T(8,128)S(1)} %apply.2.vec_0.vec_2, f32[32,128]{1,0:T(8,128)S(1)} %collective-permute-done.8.vec_1, f32[32,128]{1,0:T(8,128)S(1)} %collective-permute-done.9.vec_2, ...), custom_call_target="tpu_custom_call" | custom-call | tf_op jit(solution)/shard_map/apply/pallas_call | solution.py:687
  93.0 0.7 sums.1
  93.7 33.5 %all-gather.3 = f32[128,128]{1,0:T(8,128)S(1)} all-gather(f32[8,128]{1,0:T(8,128)S(1)} %sums.1), channel_id=5, replica_groups=mesh['city'=16,'far'=4,'near'=8] {'city'}, dimensions={0}, use_global_device_ids=true | all-gather | bytes 69632 | tf_op jit(solution)/shard_map/all_gather | solution.py:718
  127.1 0.5 basis.1
  127.6 14.7 %all-gather.4 = bf16[448,128]{1,0:T(8,128)(2,1)S(1)} all-gather(bf16[112,128]{1,0:T(8,128)(2,1)S(1)} %basis.1), channel_id=6, replica_groups=mesh['city'=16,'far'=4,'near'=8] {'far'}, dimensions={0}, use_global_device_ids=true | all-gather | bytes 143360 | tf_op jit(solution)/shard_map/all_gather | solution.py:592
  142.3 31.4 %all-gather.5 = bf16[32,112,128]{2,1,0:T(8,128)(2,1)S(1)} all-gather(bf16[4,112,128]{2,1,0:T(8,128)(2,1)S(1)} %bitcast.93), channel_id=7, replica_groups=mesh['city'=16,'far'=4,'near'=8] {'near'}, dimensions={0}, use_global_device_ids=true | all-gather | bytes 1032192 | tf_op jit(solution)/shard_map/all_gather | solution.py:592
  173.7 1.5 home.1
  175.9 0.2 conditional.2
  (5 shorter events, 0.0 us)
Async XLA Ops:
  52.1 5.6 %collective-permute-start.5 = (f32[80,128]{1,0:T(8,128)S(1)}, f32[80,128]{1,0:T(8,128)S(1)}, u32[]{:S(2)}, u32[]{:S(2)}) collective-permute-start(f32[80,128]{1,0:T(8,128)S(1)} %get-tuple-element.275.mine), channel_id=1, source_target_pairs={{1,0},{2,1},{3,2},{4,3},{5,4},{6,5},{7,6},{8,7},{9,8},{10,9},{11,1... | collective-permute-start | bytes 122888 | tf_op jit(solution)/shard_map/ppermute | solution.py:663
  54.2 4.6 %collective-permute-start.4 = (f32[80,128]{1,0:T(8,128)S(1)}, f32[80,128]{1,0:T(8,128)S(1)}, u32[]{:S(2)}, u32[]{:S(2)}) collective-permute-start(f32[80,128]{1,0:T(8,128)S(1)} %get-tuple-element.275.mine), channel_id=1, source_target_pairs={{0,1},{1,2},{2,3},{3,4},{4,5},{5,6},{6,7},{7,8},{8,9},{9,10},{10,1... | collective-permute-start | bytes 122888 | tf_op jit(solution)/shard_map/ppermute | solution.py:663
  70.2 5.6 %collective-permute-start.7 = (f32[32,128]{1,0:T(8,128)S(1)}, f32[32,128]{1,0:T(8,128)S(1)}, u32[]{:S(2)}, u32[]{:S(2)}) collective-permute-start(f32[32,128]{1,0:T(8,128)S(1)} %get-tuple-element.276.vec_0.vec_1), channel_id=1, source_target_pairs={{1,0},{2,1},{3,2},{4,3},{5,4},{6,5},{7,6},{8,7},{9,8},{10,9},{11,1... | collective-permute-start | bytes 49160 | tf_op jit(solution)/shard_map/ppermute | solution.py:663
  72.1 4.5 %collective-permute-start.6 = (f32[32,128]{1,0:T(8,128)S(1)}, f32[32,128]{1,0:T(8,128)S(1)}, u32[]{:S(2)}, u32[]{:S(2)}) collective-permute-start(f32[32,128]{1,0:T(8,128)S(1)} %get-tuple-element.276.vec_0.vec_1), channel_id=1, source_target_pairs={{0,1},{1,2},{2,3},{3,4},{4,5},{5,6},{6,7},{7,8},{8,9},{9,10},{10,1... | collective-permute-start | bytes 49160 | tf_op jit(solution)/shard_map/ppermute | solution.py:663
  81.5 5.7 %collective-permute-start.9 = (f32[32,128]{1,0:T(8,128)S(1)}, f32[32,128]{1,0:T(8,128)S(1)}, u32[]{:S(2)}, u32[]{:S(2)}) collective-permute-start(f32[32,128]{1,0:T(8,128)S(1)} %apply.2.vec_0.vec_2), channel_id=1, source_target_pairs={{1,0},{2,1},{3,2},{4,3},{5,4},{6,5},{7,6},{8,7},{9,8},{10,9},{11,1... | collective-permute-start | bytes 49160 | tf_op jit(solution)/shard_map/ppermute | solution.py:663
  83.5 4.6 %collective-permute-start.8 = (f32[32,128]{1,0:T(8,128)S(1)}, f32[32,128]{1,0:T(8,128)S(1)}, u32[]{:S(2)}, u32[]{:S(2)}) collective-permute-start(f32[32,128]{1,0:T(8,128)S(1)} %apply.2.vec_0.vec_2), channel_id=1, source_target_pairs={{0,1},{1,2},{2,3},{3,4},{4,5},{5,6},{6,7},{7,8},{8,9},{9,10},{10,1... | collective-permute-start | bytes 49160 | tf_op jit(solution)/shard_map/ppermute | solution.py:663
  87.2 88.7 %copy-start = (f32[2,65536]{1,0:T(2,128)S(1)}, f32[2,65536]{1,0:T(2,128)}, u32[]{:S(2)}) copy-start(f32[2,65536]{1,0:T(2,128)} %coords.1) | copy-start | bytes 1572868
  87.2 88.7 %copy-start.1 = (f32[2,2048]{1,0:T(2,128)S(1)}, f32[2,2048]{1,0:T(2,128)}, u32[]{:S(2)}) copy-start(f32[2,2048]{1,0:T(2,128)} %right_ref.1) | copy-start | bytes 49156
  87.2 88.7 %copy-start.2 = (f32[2048]{0:T(1024)S(1)}, f32[2048]{0:T(1024)}, u32[]{:S(2)}) copy-start(f32[2048]{0:T(1024)} %param.14) | copy-start | bytes 24580
  87.2 88.7 %copy-start.3 = (s32[1,5,3]{1,0,2:T(1,128)S(1)}, s32[1,5,3]{1,0,2:T(1,128)}, u32[]{:S(2)}) copy-start(s32[1,5,3]{1,0,2:T(1,128)} %param.17) | copy-start | bytes 184
